TPU v7x, 32 devices: a whole 2x2x4 slice. The times are simulated.
32 devices in a mesh: dp: 4 (over x, core), ctx: 8 (over z, y).
Axes of the slice: x: 2, y: 2, z: 4, core: 2. Of those that a mesh axis runs over, the one named last changes fastest.
Arguments:
- inputs: bfloat16 [32, 1024, 768], P('dp', 'ctx'), may hold values from -6 to 6
- segments: int32 [32, 1024], P('dp'), may hold values from 0 to 5, as said below
- random_blocks: int32 [32, 16, 12, 3], P('dp', 'ctx'), may hold values from 0 to 15, as said below
- cotangent: bfloat16 [32, 1024, 768], P('dp', 'ctx'), may hold values from -6 to 6
- qkv_weight: bfloat16 [768, 2304], P('dp'), may hold values from -0.21875 to 0.21875
- qv_bias: bfloat16 [1536], P('dp'), may hold values from -2 to 2
- out_weight: bfloat16 [768, 768], P('dp'), may hold values from -3.5 to 3.5
- out_bias: bfloat16 [768], P('dp'), may hold values from -2 to 2
- norm1_gain: bfloat16 [768], P('dp'), may hold values from 0.5 to 1.5
- norm1_bias: bfloat16 [768], P('dp'), may hold values from -2 to 2
- up_weight: bfloat16 [768, 3072], P('dp'), may hold values from -0.21875 to 0.21875
- up_bias: bfloat16 [3072], P('dp'), may hold values from -2 to 2
- down_weight: bfloat16 [3072, 768], P('dp'), may hold values from -0.109375 to 0.109375
- down_bias: bfloat16 [768], P('dp'), may hold values from -2 to 2
- norm2_gain: bfloat16 [768], P('dp'), may hold values from 0.5 to 1.5
- norm2_bias: bfloat16 [768], P('dp'), may hold values from -2 to 2
Outputs:
- layer_out: bfloat16 [32, 1024, 768], P('dp', 'ctx')
- input_grad: bfloat16 [32, 1024, 768], P('dp', 'ctx')
- grad_qkv_weight: float32 [768, 2304], P('dp')
- grad_qv_bias: float32 [1536], P('dp')
- grad_out_weight: float32 [768, 768], P('dp')
- grad_out_bias: float32 [768], P('dp')
- grad_norm1_gain: float32 [768], P('dp')
- grad_norm1_bias: float32 [768], P('dp')
- grad_up_weight: float32 [768, 3072], P('dp')
- grad_up_bias: float32 [3072], P('dp')
- grad_down_weight: float32 [3072, 768], P('dp')
- grad_down_bias: float32 [768], P('dp')
- grad_norm2_gain: float32 [768], P('dp')
- grad_norm2_bias: float32 [768], P('dp')
Inputs may be any that keep to these rules, and one draw needn't show every extreme that they name: `segments`: segment numbers start at 0 and never fall along a sequence. In each group of 8 sequences that share an index of dp, one sequence is a single document and another packs documents of exactly 200 tokens; the others pack documents of 200 to 2000 tokens; in every packed sequence the last document is cut by the sequence's end. `random_blocks`: for each group of 8 sequences that share an index of dp and each aligned run of 2 query blocks, the entries over those sequences, blocks, heads and slots name blocks of every aligned run of 2 key blocks exactly 72 times.
All inputs are finite; a program needn't handle non-finite values.
Results may differ from a plain program's by a relative error of at most 0.015.
Values may be sent and summed in bfloat16 or wider, within the bound.
No kernel may reach another device: no remote copies, remote signals or barrier semaphores. Data moves between devices by JAX's collectives and lax.ppermute only.
A program may use at most 576 MiB of HBM per device.

v0:
```python
import jax
import jax.numpy as jnp
from jax import lax
from jax.sharding import PartitionSpec as P

eps_norm = 1e-12
masked_score = -1e30


def spread_2(value, axis, source):
    kept = jnp.where(lax.axis_index(axis) == source, value, 0).astype(value.dtype)
    return lax.psum(kept, axis)


def padded(cells, sides, width):
    for axis, dim in sides:
        count = lax.axis_size(axis)
        ends = count - 1
        head = lax.slice_in_dim(cells, 0, width, axis=dim)
        tail = lax.slice_in_dim(cells, cells.shape[dim] - width, cells.shape[dim], axis=dim)
        cells = jnp.concatenate(
            [
                lax.ppermute(tail, axis, [(i, (i + 1) % count) for i in range(ends)]),
                cells,
                lax.ppermute(head, axis, [((i + 1) % count, i) for i in range(ends)]),
            ],
            axis=dim,
        )
    return cells


def combined_all(value, axis, join):
    pieces = jax.tree.map(lambda part: lax.all_gather(part, axis), value)
    head = jax.tree.map(lambda part: part[0], pieces)
    tail = jax.tree.map(lambda part: part[1:], pieces)
    running, _ = lax.scan(lambda running, piece: (join(running, piece), None), head, tail)
    return running


def exact_gelu(values_in):
    return jax.nn.gelu(values_in, approximate=False)


def norm_forward(values_in, gain_vec, offset_vec):
    centred = values_in - jnp.mean(values_in, axis=-1, keepdims=True)
    inverse = lax.rsqrt(jnp.mean(centred * centred, axis=-1, keepdims=True) + eps_norm)
    normed = centred * inverse
    return (normed * gain_vec + offset_vec, normed, inverse)


def norm_backward(incoming, normed, inverse, gain_vec):
    scaled = incoming * gain_vec
    centred_grad = (
        scaled
        - jnp.mean(scaled, axis=-1, keepdims=True)
        - normed * jnp.mean(scaled * normed, axis=-1, keepdims=True)
    )
    return (centred_grad * inverse, jnp.sum(incoming * normed, axis=0), jnp.sum(incoming, axis=0))


def fetch_weights(
    qkv_weight,
    qv_bias,
    out_weight,
    out_bias,
    norm1_gain,
    norm1_bias,
    up_weight,
    up_bias,
    down_weight,
    down_bias,
    norm2_gain,
    norm2_bias,
):
    return (
        lax.all_gather(qkv_weight, "dp", axis=0, tiled=True),
        lax.all_gather(qv_bias, "dp", axis=0, tiled=True),
        lax.all_gather(out_weight, "dp", axis=0, tiled=True),
        lax.all_gather(out_bias, "dp", axis=0, tiled=True),
        lax.all_gather(norm1_gain, "dp", axis=0, tiled=True),
        lax.all_gather(norm1_bias, "dp", axis=0, tiled=True),
        lax.all_gather(up_weight, "dp", axis=0, tiled=True),
        lax.all_gather(up_bias, "dp", axis=0, tiled=True),
        lax.all_gather(down_weight, "dp", axis=0, tiled=True),
        lax.all_gather(down_bias, "dp", axis=0, tiled=True),
        lax.all_gather(norm2_gain, "dp", axis=0, tiled=True),
        lax.all_gather(norm2_bias, "dp", axis=0, tiled=True),
    )


def spread(rows, root):
    return spread_2(rows, "ctx", root)


def spread_grad(rows, root):
    return spread_2(rows, "ctx", root)


def join_stats(first, second):
    top = jnp.maximum(first[0], second[0])
    return (top, first[1] * jnp.exp(first[0] - top) + second[1] * jnp.exp(second[0] - top))


def slab_view(tokens_kv, block_len, head_count):
    leading_dims = tokens_kv.shape[:-2]
    length, pair_width = tokens_kv.shape[-2:]
    half_width = pair_width // (2 * head_count)
    depth = len(leading_dims)
    parted = tokens_kv.reshape(
        leading_dims + (length // block_len, block_len, 2, head_count, half_width)
    )
    perm_axes = tuple(range(depth)) + (depth, depth + 3, depth + 1, depth + 2, depth + 4)
    return parted.transpose(perm_axes).reshape(
        leading_dims + (length // block_len, head_count, block_len, 2 * half_width)
    )


def token_view(slabs):
    leading_dims = slabs.shape[:-4]
    block_count, head_count, block_len, slab_width = slabs.shape[-4:]
    half_width = slab_width // 2
    depth = len(leading_dims)
    parted = slabs.reshape(leading_dims + (block_count, head_count, block_len, 2, half_width))
    perm_axes = tuple(range(depth)) + (depth, depth + 2, depth + 3, depth + 1, depth + 4)
    return parted.transpose(perm_axes).reshape(
        leading_dims + (block_count * block_len, 2 * head_count * half_width)
    )


def split_lead(member, group_count):
    return member.reshape((group_count, member.shape[0] // group_count) + member.shape[1:])


def place_rows(block_rows, tok_rows):
    half_rows = block_rows.shape[1] // 2
    middle = jnp.zeros(
        (block_rows.shape[0], tok_rows - 2 * half_rows) + block_rows.shape[2:], block_rows.dtype
    )
    return jnp.concatenate([block_rows[:, :half_rows], middle, block_rows[:, half_rows:]], axis=1)


def collect(key_value, query_rows, send_ids, block_len, head_count):
    width = query_rows.shape[-1]
    extended = padded(key_value, (("ctx", 1),), block_len)
    first_rows = spread(
        jnp.concatenate([query_rows[:, :block_len], key_value[:, :block_len]], axis=2), 0
    )
    last_rows = spread(
        jnp.concatenate([query_rows[:, -block_len:], key_value[:, -block_len:]], axis=2),
        lax.axis_size("ctx") - 1,
    )
    leading = jnp.concatenate([first_rows[..., width:], last_rows[..., width:]], axis=1)
    global_q = jnp.concatenate([first_rows[..., :width], last_rows[..., :width]], axis=1)
    slab_table = slab_view(key_value, block_len, head_count)
    slab_table = slab_table.reshape((-1,) + slab_table.shape[-2:])
    wanted = lax.all_to_all(send_ids, "ctx", split_axis=0, concat_axis=0, tiled=True)
    looked_up = jnp.take(slab_table, wanted, axis=0)
    fetched = lax.all_to_all(looked_up, "ctx", split_axis=0, concat_axis=0, tiled=True)
    return (extended, leading, global_q, fetched, wanted)


def arrange(fetched, unsorting, list_shape):
    flat_slabs = fetched.reshape((-1,) + fetched.shape[-2:])
    return jnp.take(flat_slabs, unsorting, axis=0).reshape(list_shape + fetched.shape[-2:])


def key_slabs(extended, leading, randoms):
    seq_count, per_dev, head_count = randoms.shape[:3]
    block_len, slab_width = randoms.shape[-2:]
    near_slabs = slab_view(extended, block_len, head_count)
    lead_slabs = slab_view(leading, block_len, head_count)
    nearby = jnp.stack([near_slabs[:, offset : offset + per_dev] for offset in range(3)], axis=3)
    global_part = jnp.broadcast_to(
        lead_slabs.transpose(0, 2, 1, 3, 4)[:, None],
        (seq_count, per_dev, head_count, 2, block_len, slab_width),
    )
    return jnp.concatenate([nearby, global_part, randoms], axis=3)


def masked_scores(queries, key_part, key_seg, present, query_seg):
    score_scale = queries.shape[-1] ** (-0.5)
    scores = (
        jnp.einsum("spqhd,sphkjd->sphqkj", queries, key_part, preferred_element_type=jnp.float32)
        * score_scale
    )
    allowed = present[:, :, :, None, :, None] & (
        key_seg[:, :, :, None, :, :] == query_seg[:, :, None, :, None, None]
    )
    scores = jnp.where(allowed, scores, masked_score)
    return scores.reshape(scores.shape[:4] + (-1,))


def global_scores(global_q, keys_local, global_seg, local_seg):
    score_scale = global_q.shape[-1] ** (-0.5)
    scores = (
        jnp.einsum("sqhd,skhd->shqk", global_q, keys_local, preferred_element_type=jnp.float32)
        * score_scale
    )
    allowed = global_seg[:, None, :, None] == local_seg[:, None, None, :]
    return (jnp.where(allowed, scores, masked_score), allowed)


def attend_forward(members):
    queries, extended, leading, randoms, key_seg, present, query_seg = members
    head_size = queries.shape[-1]
    slabs = key_slabs(extended, leading, randoms)
    scores = masked_scores(queries, slabs[..., :head_size], key_seg, present, query_seg)
    row_max = jnp.max(scores, axis=-1, keepdims=True)
    raw_weights = jnp.exp(scores - row_max)
    denominator = jnp.sum(raw_weights, axis=-1, keepdims=True)
    softmax_w = (raw_weights / denominator).astype(jnp.bfloat16)
    val_part = slabs[..., head_size:].reshape(scores.shape[:3] + (-1, head_size))
    attended = jnp.einsum(
        "sphqn,sphnd->spqhd", softmax_w, val_part, preferred_element_type=jnp.float32
    )
    return (attended.astype(jnp.bfloat16), (row_max + jnp.log(denominator))[..., 0])


def attend_backward(members):
    queries, extended, leading, randoms, key_seg, present, query_seg, log_total, grad_att = members
    head_size = queries.shape[-1]
    score_scale = head_size ** (-0.5)
    slabs = key_slabs(extended, leading, randoms)
    scores = masked_scores(queries, slabs[..., :head_size], key_seg, present, query_seg)
    softmax_f = jnp.exp(scores - log_total[..., None])
    flat_shape = scores.shape[:3] + (-1, head_size)
    key_flat = slabs[..., :head_size].reshape(flat_shape)
    val_flat = slabs[..., head_size:].reshape(flat_shape)
    grad_weights = jnp.einsum(
        "spqhd,sphnd->sphqn", grad_att, val_flat, preferred_element_type=jnp.float32
    )
    row_inner = jnp.sum(softmax_f * grad_weights, axis=-1, keepdims=True)
    grad_scores = (softmax_f * (grad_weights - row_inner)).astype(jnp.bfloat16)
    grad_queries = (
        jnp.einsum("sphqn,sphnd->spqhd", grad_scores, key_flat, preferred_element_type=jnp.float32)
        * score_scale
    )
    grad_keys = (
        jnp.einsum("sphqn,spqhd->sphnd", grad_scores, queries, preferred_element_type=jnp.float32)
        * score_scale
    )
    grad_values = jnp.einsum(
        "sphqn,spqhd->sphnd",
        softmax_f.astype(jnp.bfloat16),
        grad_att,
        preferred_element_type=jnp.float32,
    )
    slab_shape = slabs.shape[:-1] + (head_size,)
    grad_slabs = jnp.concatenate(
        [grad_keys.reshape(slab_shape), grad_values.reshape(slab_shape)], axis=-1
    )
    no_pad = (0, 0)
    near_grad = jnp.pad(grad_slabs[:, :, :, 0], (no_pad, (0, 2), no_pad, no_pad, no_pad))
    near_grad = near_grad + jnp.pad(
        grad_slabs[:, :, :, 1], (no_pad, (1, 1), no_pad, no_pad, no_pad)
    )
    near_grad = near_grad + jnp.pad(
        grad_slabs[:, :, :, 2], (no_pad, (2, 0), no_pad, no_pad, no_pad)
    )
    global_grad = jnp.sum(grad_slabs[:, :, :, 3:5], axis=1).transpose(0, 2, 1, 3, 4)
    return (grad_queries, token_view(near_grad), token_view(global_grad), grad_slabs[:, :, :, 5:])


def body(
    inputs,
    segments,
    random_blocks,
    cotangent,
    qkv_weight,
    qv_bias,
    out_weight,
    out_bias,
    norm1_gain,
    norm1_bias,
    up_weight,
    up_bias,
    down_weight,
    down_bias,
    norm2_gain,
    norm2_bias,
):
    seq_count, tok_rows, width = inputs.shape
    per_dev, head_count, rand_count = random_blocks.shape[1:]
    block_len = tok_rows // per_dev
    head_size = width // head_count
    block_total = segments.shape[1] // block_len
    ctx_count = lax.axis_size("ctx")
    ctx_index = lax.axis_index("ctx")
    tok_count = seq_count * tok_rows
    group_count = seq_count * per_dev // 8
    gathered = fetch_weights(
        qkv_weight,
        qv_bias,
        out_weight,
        out_bias,
        norm1_gain,
        norm1_bias,
        up_weight,
        up_bias,
        down_weight,
        down_bias,
        norm2_gain,
        norm2_bias,
    )
    (
        weight_qkv,
        bias_qv,
        weight_out,
        bias_out,
        gain_one,
        shift_one,
        weight_up,
        bias_up,
        weight_down,
        bias_down,
        gain_two,
        shift_two,
    ) = gathered
    owners = random_blocks // per_dev
    seq_grid = jnp.arange(seq_count, dtype=jnp.int32)[:, None, None, None]
    head_grid = jnp.arange(head_count, dtype=jnp.int32)[None, None, :, None]
    payload = ((seq_grid * per_dev + random_blocks % per_dev) * head_count + head_grid).reshape(-1)
    sorting = jnp.argsort(owners.reshape(-1), stable=True)
    unsorting = jnp.argsort(sorting, stable=True)
    send_ids = jnp.take(payload, sorting).reshape(ctx_count, -1)
    first_block = ctx_index * per_dev + jnp.arange(per_dev, dtype=jnp.int32)
    fixed_lists = jnp.stack(
        [
            first_block - 1,
            first_block,
            first_block + 1,
            first_block * 0,
            first_block * 0 + block_total - 1,
        ],
        axis=1,
    )
    key_index = jnp.concatenate(
        [
            jnp.broadcast_to(fixed_lists[None, :, None, :], (seq_count, per_dev, head_count, 5)),
            random_blocks,
        ],
        axis=3,
    )
    present = (key_index >= 0) & (key_index < block_total)
    clipped = jnp.clip(key_index, 0, block_total - 1)
    seg_blocks = segments.reshape(seq_count, block_total, block_len)
    key_seg = seg_blocks[seq_grid, clipped]
    local_seg = lax.dynamic_slice_in_dim(segments, ctx_index * tok_rows, tok_rows, 1)
    query_seg = local_seg.reshape(seq_count, per_dev, block_len)
    global_seg = jnp.concatenate([segments[:, :block_len], segments[:, -block_len:]], axis=1)
    row_ids = jnp.arange(tok_rows, dtype=jnp.int32)
    global_mask = (
        (ctx_index == 0) & (row_ids < block_len)
        | (ctx_index == ctx_count - 1) & (row_ids >= tok_rows - block_len)
    )[None, :, None]
    flat_x = inputs.reshape(tok_count, width)
    projected = jnp.dot(flat_x, weight_qkv, preferred_element_type=jnp.float32)
    queries = (projected[:, :width] + bias_qv[:width]).astype(jnp.bfloat16)
    key_value = jnp.concatenate(
        [projected[:, width : 2 * width], projected[:, 2 * width :] + bias_qv[width:]], axis=1
    )
    key_value = key_value.astype(jnp.bfloat16).reshape(seq_count, tok_rows, 2 * width)
    query_rows = queries.reshape(seq_count, tok_rows, width)
    extended, leading, global_q, fetched, received = collect(
        key_value, query_rows, send_ids, block_len, head_count
    )
    randoms = arrange(fetched, unsorting, random_blocks.shape)
    query_blocks = queries.reshape(seq_count, per_dev, block_len, head_count, head_size)
    members = tuple(
        (
            split_lead(member, group_count)
            for member in (query_blocks, extended, leading, randoms, key_seg, present, query_seg)
        )
    )
    attended, log_total = lax.map(attend_forward, members)
    attended = attended.reshape(seq_count, tok_rows, width)
    keys_local = key_value[..., :width].reshape(seq_count, tok_rows, head_count, head_size)
    vals_local = key_value[..., width:].reshape(seq_count, tok_rows, head_count, head_size)
    global_heads = global_q.reshape(seq_count, 2 * block_len, head_count, head_size)
    wide_scores, wide_allowed = global_scores(global_heads, keys_local, global_seg, local_seg)
    local_top = jnp.max(wide_scores, axis=-1)
    local_total = jnp.sum(
        jnp.where(wide_allowed, jnp.exp(wide_scores - local_top[..., None]), 0.0), axis=-1
    )
    top, total = combined_all((local_top, local_total), "ctx", join_stats)
    global_lse = top + jnp.log(total)
    wide_probs = jnp.exp(wide_scores - global_lse[..., None])
    partial_mix = jnp.einsum(
        "shqk,skhd->sqhd",
        wide_probs.astype(jnp.bfloat16),
        vals_local,
        preferred_element_type=jnp.float32,
    )
    global_att = (
        lax.psum(partial_mix, "ctx").astype(jnp.bfloat16).reshape(seq_count, 2 * block_len, width)
    )
    attended = jnp.where(global_mask, place_rows(global_att, tok_rows), attended).reshape(
        tok_count, width
    )
    branch = jnp.dot(attended, weight_out, preferred_element_type=jnp.float32) + bias_out
    hidden, normed_one, inverse_one = norm_forward(flat_x + branch, gain_one, shift_one)
    hidden_low = hidden.astype(jnp.bfloat16)
    up_proj = jnp.dot(hidden_low, weight_up, preferred_element_type=jnp.float32) + bias_up
    active, gelu_back = jax.vjp(exact_gelu, up_proj)
    active_low = active.astype(jnp.bfloat16)
    mlp_out = jnp.dot(active_low, weight_down, preferred_element_type=jnp.float32) + bias_down
    result, normed_two, inverse_two = norm_forward(hidden + mlp_out, gain_two, shift_two)
    gathered = fetch_weights(
        qkv_weight,
        qv_bias,
        out_weight,
        out_bias,
        norm1_gain,
        norm1_bias,
        up_weight,
        up_bias,
        down_weight,
        down_bias,
        norm2_gain,
        norm2_bias,
    )
    (
        weight_qkv,
        bias_qv,
        weight_out,
        bias_out,
        gain_one,
        shift_one,
        weight_up,
        bias_up,
        weight_down,
        bias_down,
        gain_two,
        shift_two,
    ) = gathered
    grad_result = cotangent.reshape(tok_count, width).astype(jnp.float32)
    grad_sum, grad_gain_two, grad_shift_two = norm_backward(
        grad_result, normed_two, inverse_two, gain_two
    )
    grad_mlp = grad_sum.astype(jnp.bfloat16)
    grad_down_w = jnp.dot(active_low.T, grad_mlp, preferred_element_type=jnp.float32)
    grad_down_b = jnp.sum(grad_mlp, axis=0, dtype=jnp.float32)
    grad_active = jnp.dot(grad_mlp, weight_down.T, preferred_element_type=jnp.float32)
    grad_upper = gelu_back(grad_active)[0].astype(jnp.bfloat16)
    grad_up_w = jnp.dot(hidden_low.T, grad_upper, preferred_element_type=jnp.float32)
    grad_up_b = jnp.sum(grad_upper, axis=0, dtype=jnp.float32)
    grad_hidden = grad_sum + jnp.dot(grad_upper, weight_up.T, preferred_element_type=jnp.float32)
    grad_pre, grad_gain_one, grad_shift_one = norm_backward(
        grad_hidden, normed_one, inverse_one, gain_one
    )
    grad_branch = grad_pre.astype(jnp.bfloat16)
    grad_out_w = jnp.dot(attended.T, grad_branch, preferred_element_type=jnp.float32)
    grad_out_b = jnp.sum(grad_branch, axis=0, dtype=jnp.float32)
    grad_rows = (
        jnp.dot(grad_branch, weight_out.T, preferred_element_type=jnp.float32)
        .astype(jnp.bfloat16)
        .reshape(seq_count, tok_rows, width)
    )
    cot_first = spread_grad(grad_rows[:, :block_len], 0)
    cot_last = spread_grad(grad_rows[:, -block_len:], ctx_count - 1)
    sparse_grad = jnp.where(global_mask, jnp.zeros((), jnp.bfloat16), grad_rows)
    grad_att = sparse_grad.reshape(group_count, -1, per_dev, block_len, head_count, head_size)
    extended, leading, global_q, fetched, received = collect(
        key_value, query_rows, send_ids, block_len, head_count
    )
    randoms = arrange(fetched, unsorting, random_blocks.shape)
    global_heads = global_q.reshape(seq_count, 2 * block_len, head_count, head_size)
    back_members = tuple(
        (
            split_lead(member, group_count)
            for member in (query_blocks, extended, leading, randoms, key_seg, present, query_seg)
        )
    ) + (log_total, grad_att)
    grad_queries, near_grad, global_grad, rand_grad = lax.map(attend_backward, back_members)
    wide_scores, wide_allowed = global_scores(global_heads, keys_local, global_seg, local_seg)
    wide_probs = jnp.exp(wide_scores - global_lse[..., None])
    global_cot = jnp.concatenate([cot_first, cot_last], axis=1).reshape(
        seq_count, 2 * block_len, head_count, head_size
    )
    wide_dprob = jnp.einsum(
        "sqhd,skhd->shqk", global_cot, vals_local, preferred_element_type=jnp.float32
    )
    wide_inner = lax.psum(jnp.sum(wide_probs * wide_dprob, axis=-1), "ctx")
    wide_dscore = (wide_probs * (wide_dprob - wide_inner[..., None])).astype(jnp.bfloat16)
    score_scale = head_size ** (-0.5)
    global_q_part = (
        jnp.einsum("shqk,skhd->sqhd", wide_dscore, keys_local, preferred_element_type=jnp.float32)
        * score_scale
    ).reshape(seq_count, 2 * block_len, width)
    wide_key_grad = (
        jnp.einsum("shqk,sqhd->skhd", wide_dscore, global_heads, preferred_element_type=jnp.float32)
        * score_scale
    )
    wide_val_grad = jnp.einsum(
        "shqk,sqhd->skhd",
        wide_probs.astype(jnp.bfloat16),
        global_cot,
        preferred_element_type=jnp.float32,
    )
    wide_pair = jnp.concatenate(
        [
            wide_key_grad.reshape(seq_count, tok_rows, width),
            wide_val_grad.reshape(seq_count, tok_rows, width),
        ],
        axis=2,
    )
    near_grad = near_grad.reshape((seq_count,) + near_grad.shape[2:])
    middle = jnp.zeros((seq_count, tok_rows - 2 * block_len, 2 * width), jnp.float32)
    rims = jnp.concatenate([near_grad[:, :block_len], middle, near_grad[:, -block_len:]], axis=1)
    arrived = padded(rims.astype(jnp.bfloat16), (("ctx", 1),), block_len).astype(rims.dtype)
    pair_grad = (
        near_grad[:, block_len : block_len + tok_rows]
        + jnp.concatenate([arrived[:, :block_len], middle, arrived[:, -block_len:]], axis=1)
        + wide_pair
    )
    global_grad = global_grad.reshape((seq_count,) + global_grad.shape[2:])
    global_sum, query_sum = lax.psum((global_grad, global_q_part), "ctx")
    pair_grad = pair_grad + jnp.where(global_mask, place_rows(global_sum, tok_rows), 0.0)
    slab_shape = rand_grad.shape[-2:]
    outgoing = jnp.take(rand_grad.reshape((-1,) + slab_shape), sorting, axis=0).reshape(
        (ctx_count, -1) + slab_shape
    )
    returned = lax.all_to_all(
        outgoing.astype(jnp.bfloat16), "ctx", split_axis=0, concat_axis=0, tiled=True
    ).astype(outgoing.dtype)
    owned = jax.ops.segment_sum(
        returned.reshape((-1,) + slab_shape),
        received.reshape(-1),
        num_segments=seq_count * per_dev * head_count,
    )
    pair_grad = pair_grad + token_view(owned.reshape((seq_count, per_dev, head_count) + slab_shape))
    query_full = grad_queries.reshape(seq_count, tok_rows, width) + jnp.where(
        global_mask, place_rows(query_sum, tok_rows), 0.0
    )
    query_grad = query_full.reshape(tok_count, width).astype(jnp.bfloat16)
    kv_grad = pair_grad.reshape(tok_count, 2 * width).astype(jnp.bfloat16)
    grad_proj = jnp.concatenate([query_grad, kv_grad], axis=1)
    grad_qkv_w = jnp.dot(flat_x.T, grad_proj, preferred_element_type=jnp.float32)
    grad_qv_b = jnp.concatenate(
        [
            jnp.sum(query_grad, axis=0, dtype=jnp.float32),
            jnp.sum(kv_grad[:, width:], axis=0, dtype=jnp.float32),
        ]
    )
    grad_input = grad_pre + jnp.dot(grad_proj, weight_qkv.T, preferred_element_type=jnp.float32)
    shares = (
        lax.psum_scatter(
            grad_qkv_w.astype(jnp.bfloat16), "dp", scatter_dimension=0, tiled=True
        ).astype(jnp.float32),
        lax.psum_scatter(
            grad_qv_b.astype(jnp.bfloat16), "dp", scatter_dimension=0, tiled=True
        ).astype(jnp.float32),
        lax.psum_scatter(
            grad_out_w.astype(jnp.bfloat16), "dp", scatter_dimension=0, tiled=True
        ).astype(jnp.float32),
        lax.psum_scatter(
            grad_out_b.astype(jnp.bfloat16), "dp", scatter_dimension=0, tiled=True
        ).astype(jnp.float32),
        lax.psum_scatter(
            grad_gain_one.astype(jnp.bfloat16), "dp", scatter_dimension=0, tiled=True
        ).astype(jnp.float32),
        lax.psum_scatter(
            grad_shift_one.astype(jnp.bfloat16), "dp", scatter_dimension=0, tiled=True
        ).astype(jnp.float32),
        lax.psum_scatter(
            grad_up_w.astype(jnp.bfloat16), "dp", scatter_dimension=0, tiled=True
        ).astype(jnp.float32),
        lax.psum_scatter(
            grad_up_b.astype(jnp.bfloat16), "dp", scatter_dimension=0, tiled=True
        ).astype(jnp.float32),
        lax.psum_scatter(
            grad_down_w.astype(jnp.bfloat16), "dp", scatter_dimension=0, tiled=True
        ).astype(jnp.float32),
        lax.psum_scatter(
            grad_down_b.astype(jnp.bfloat16), "dp", scatter_dimension=0, tiled=True
        ).astype(jnp.float32),
        lax.psum_scatter(
            grad_gain_two.astype(jnp.bfloat16), "dp", scatter_dimension=0, tiled=True
        ).astype(jnp.float32),
        lax.psum_scatter(
            grad_shift_two.astype(jnp.bfloat16), "dp", scatter_dimension=0, tiled=True
        ).astype(jnp.float32),
    )
    totals = lax.psum(
        (
            shares[0],
            shares[1],
            shares[2],
            shares[3],
            shares[4],
            shares[5],
            shares[6],
            shares[7],
            shares[8],
            shares[9],
            shares[10],
            shares[11],
        ),
        "ctx",
    )
    return (
        result.astype(jnp.bfloat16).reshape(inputs.shape),
        grad_input.astype(jnp.bfloat16).reshape(inputs.shape),
        totals[0],
        totals[1],
        totals[2],
        totals[3],
        totals[4],
        totals[5],
        totals[6],
        totals[7],
        totals[8],
        totals[9],
        totals[10],
        totals[11],
    )


def solution(mesh):
    placed = (
        P("dp", "ctx", None),
        P("dp", None),
        P("dp", "ctx", None, None),
        P("dp", "ctx", None),
        P("dp", None),
        P("dp"),
        P("dp", None),
        P("dp"),
        P("dp"),
        P("dp"),
        P("dp", None),
        P("dp"),
        P("dp", None),
        P("dp"),
        P("dp"),
        P("dp"),
    )
    return jax.shard_map(
        body,
        mesh=mesh,
        in_specs=placed,
        out_specs=(
            P("dp", "ctx", None),
            P("dp", "ctx", None),
            P("dp", None),
            P("dp"),
            P("dp", None),
            P("dp"),
            P("dp"),
            P("dp"),
            P("dp", None),
            P("dp"),
            P("dp", None),
            P("dp"),
            P("dp"),
            P("dp"),
        ),
        check_vma=False,
    )
```

profile of v0, /device:TPU:0, one launch (start us, length us, event | category | flops | bytes accessed | tf_op | source)
XLA Modules:
  0.0 3095.9 jit_solution(16595840193974657980)
XLA Ops:
  14.8 28.3 all-gather.9.cloned.1.call-done
  90.2 21.4 copy.288
  121.4 18.1 gather_fusion.3
  189.0 17.1 gather_fusion.1
  229.2 55.9 %collective-permute-done = bf16[8,64,1536]{2,1,0:T(8,128)(2,1)} collective-permute-done((bf16[8,64,1536]{2,1,0:T(8,128)(2,1)}, bf16[8,64,1536]{2,1,0:T(8,128)(2,1)}, u32[]{:S(2)}, u32[]{:S(2)}) %collective-permute-start) | collective-permute-done | bytes 1572896 | tf_op jit(solution)/shard_map/ppermute | solution.py:23
  301.5 91.5 %all-reduce.33.cloned.1.call-done = (bf16[8,64,2304]{2,1,0:T(8,128)(2,1)}, bf16[8,64,2304]{2,1,0:T(8,128)(2,1)}) async-done(((bf16[8,64,2304]{2,1,0:T(8,128)(2,1)}, bf16[8,64,2304]{2,1,0:T(8,128)(2,1)}), (bf16[8,64,2304]{2,1,0:T(8,128)(2,1)}, bf16[8,64,2304]{2,1,0:T(8,128)(2,1)})) %all-reduce.33.cloned.1.call-update) | async-done | bytes 4718608 | tf_op jit(solution)/shard_map/psum | solution.py:12
  414.0 101.5 %all-gather.1 = f32[64,12,128]{2,0,1:T(8,128)S(1)} all-gather(f32[8,12,128]{2,0,1:T(8,128)S(1)} %copy.272), channel_id=3, replica_groups=mesh['dp'=4,'ctx'=8] {'ctx'}, dimensions={0}, use_global_device_ids=true | all-gather | bytes 442368 | tf_op jit(solution)/shard_map/all_gather | solution.py:33
  515.5 31.0 %all-gather = f32[64,12,128]{2,0,1:T(8,128)S(1)} all-gather(f32[8,12,128]{2,0,1:T(8,128)S(1)} %copy.271), channel_id=2, replica_groups=mesh['dp'=4,'ctx'=8] {'ctx'}, dimensions={0}, use_global_device_ids=true | all-gather | bytes 442368 | tf_op jit(solution)/shard_map/all_gather | solution.py:33
  560.8 114.8 %all-reduce.34 = bf16[8,128,12,64]{1,3,2,0:T(8,128)(2,1)} all-reduce(f32[8,128,12,64]{1,3,2,0:T(8,128)} %convolution_bitcast_fusion), channel_id=1, replica_groups=mesh['dp'=4,'ctx'=8] {'ctx'}, use_global_device_ids=true, to_apply=%region_6.7 | all-reduce | flops 786432 | bytes 4718592 | tf_op jit(solution)/shard_map/psum | solution.py:395
  679.4 23.3 gather_fusion.4
  712.8 249.0 %while.46 = (s32[]{:T(128)}, bf16[2,4,2,64,12,64]{3,2,1,0,5,4:T(2,128)(2,1)}, f32[2,4,2,12,64]{4,3,2,1,0:T(8,128)}, bf16[2,4,256,1536]{2,3,1,0:T(8,128)(2,1)}, b...) while((s32[]{:T(128)}, ...), condition=%wide.region_12.15_spmd.clone, body=%wide.region_9.14_spmd.sunk.clone | while | flops 837150720 | bytes 250288192 | solution.py:375
  742.5 17.5 copy.437
  783.7 11.8 fusion.190
  804.5 18.7 copy.439
  823.2 11.3 fusion.191
  866.8 17.5 copy.437
  908.0 11.8 fusion.190
  928.8 18.7 copy.439
  947.5 11.3 fusion.191
  977.2 38.0 %multiply_convert_fusion.1 = (bf16[1024,3072]{1,0:T(8,128)(2,1)}, f32[1024,3072]{1,0:T(8,128)}, f32[1024,3072]{1,0:T(8,128)}) fusion(f32[3072]{0:T(1024)S(1)} %bitcast.496, bf16[768,3072]{1,0:T(8,128)(2,1)} %all-gather.13.cloned.1.call-done, f32[1024,768]{1,0:T(8,128)} %copy-done.31, f32[768]{0:T(1024)S(1)} %copy-done.82, f32[768]{0:T(1024)S(1)} %copy-done.72, ...), kind=kOutput, calls=%fused_computation.89 | convolution fusion | flops 5043388416 | bytes 39348224 | tf_op jit(solution)/shard_map/dot_general | solution.py:403
  1030.4 19.5 fusion.100
  1078.8 922.3 %while.47 = (s32[]{:T(128)}, f32[2,4,2,64,12,64]{3,2,5,4,1,0:T(2,128)}, f32[2,4,256,1536]{2,3,1,0:T(8,128)}, f32[2,4,128,1536]{2,3,1,0:T(8,128)}, bf16[2,4,2,12,...) while((s32[]{:T(128)}, ...), condition=%wide.region_24.27_spmd.clone, body=%wide.region_21.26_spmd.sunk.clone | while | flops 2061625344 | bytes 611059520 | solution.py:474
  1117.7 17.6 copy.442
  1159.4 19.8 multiply_select_fusion.5
  1179.2 28.9 copy.444
  1208.1 21.0 reshape.659
  1237.7 18.8 reshape.661
  1256.6 19.5 fusion.206
  1276.0 14.1 multiply_reduce_fusion.9
  1316.8 18.8 reshape.660
  1335.6 17.2 constant_dynamic-update-slice_fusion.15
  1352.8 17.3 constant_dynamic-update-slice_fusion.16
  1370.1 24.5 slice_reduce_fusion.4
  1405.4 22.9 slice_bitcast_fusion.11
  1428.3 53.2 %fusion.208 = (f32[4,2,12,1,64,128]{4,3,5,2,1,0:T(1,128)}, f32[4,2,12,1,64,128]{4,3,5,2,1,0:T(1,128)}, f32[4,2,12,1,64,128]{4,3,5,2,1,0:T(1,128)}) fusion(f32[4,2,12,8,64,128]{4,3,5,2,1,0:T(8,128)} %constant_dynamic-update-slice_fusion.16), kind=kLoop, calls=%fused_computation.256.clone.1.clone | loop fusion | bytes 18874368 | tf_op jit(solution)/shard_map/while/body/eval_jaxpr/slice | solution.py:253
  1481.5 17.2 copy.448
  1515.8 12.6 broadcast_in_dim.341
  1576.4 17.5 copy.442
  1618.0 20.1 multiply_select_fusion.5
  1638.1 28.9 copy.444
  1667.0 21.0 reshape.659
  1696.6 18.8 reshape.661
  1715.5 19.5 fusion.206
  1734.9 13.8 multiply_reduce_fusion.9
  1775.5 18.8 reshape.660
  1794.3 17.2 constant_dynamic-update-slice_fusion.15
  1811.5 17.4 constant_dynamic-update-slice_fusion.16
  1828.9 24.5 slice_reduce_fusion.4
  1864.2 22.9 slice_bitcast_fusion.11
  1887.1 53.2 %fusion.208 = (f32[4,2,12,1,64,128]{4,3,5,2,1,0:T(1,128)}, f32[4,2,12,1,64,128]{4,3,5,2,1,0:T(1,128)}, f32[4,2,12,1,64,128]{4,3,5,2,1,0:T(1,128)}) fusion(f32[4,2,12,8,64,128]{4,3,5,2,1,0:T(8,128)} %constant_dynamic-update-slice_fusion.16), kind=kLoop, calls=%fused_computation.256.clone.1.clone | loop fusion | bytes 18874368 | tf_op jit(solution)/shard_map/while/body/eval_jaxpr/slice | solution.py:253
  1940.3 17.2 copy.448
  1974.6 12.6 broadcast_in_dim.341
  2012.1 35.4 %psum.151 = f32[8,12,128]{2,1,0:T(8,128)S(1)} all-reduce(f32[8,12,128]{2,1,0:T(8,128)S(1)} %get-tuple-element.632), channel_id=1, replica_groups=mesh['dp'=4,'ctx'=8] {'ctx'}, use_global_device_ids=true, to_apply=%region_28.31 | all-reduce | flops 12288 | bytes 98304 | tf_op jit(solution)/shard_map/psum | solution.py:483
  2057.8 24.8 gather_fusion.2
  2161.3 40.0 %collective-permute-done.3 = bf16[8,64,1536]{2,1,0:T(8,128)(2,1)} collective-permute-done((bf16[8,64,1536]{2,1,0:T(8,128)(2,1)}, bf16[8,64,1536]{2,1,0:T(8,128)(2,1)}, u32[]{:S(2)}, u32[]{:S(2)}) %collective-permute-start.3) | collective-permute-done | bytes 1572896 | tf_op jit(solution)/shard_map/ppermute | solution.py:25
  2236.5 11.0 fusion.93
  2247.5 306.4 %all-reduce.29.cloned.1.call-done = (f32[8,128,1536]{1,2,0:T(8,128)}, f32[8,128,768]{1,2,0:T(8,128)}) async-done(((f32[8,128,1536]{1,2,0:T(8,128)}, f32[8,128,768]{1,2,0:T(8,128)}), (f32[8,128,1536]{1,2,0:T(8,128)}, f32[8,128,768]{1,2,0:T(8,128)})) %all-reduce.29.cloned.1.call-update) | async-done | bytes 9437200 | tf_op jit(solution)/shard_map/psum | solution.py:517
  2560.0 13.0 bitcast_convert_fusion
  2576.5 91.1 %scatter_fusion = f32[192,64,128]{2,1,0:T(8,128)} fusion(f32[192,64,128]{2,1,0:T(8,128)} %broadcast_in_dim.276, s32[576]{0:T(1024)S(1)} %reshape.539, f32[576,64,128]{2,1,0:T(8,128)} %bitcast_convert_fusion), kind=kCustom, calls=%fused_computation.5 | custom fusion | flops 4718592 | bytes 56625408 | tf_op jit(solution)/shard_map/scatter-add | solution.py:526
  2667.6 13.3 reshape_reshape.25
  2680.9 22.9 copy.311
  2703.8 12.7 reshape.494
  2716.5 15.3 fusion.44
  2786.5 300.9 %all-reduce.35 = (f32[192,2304]{0,1:T(8,128)S(1)}, f32[384]{0:T(512)}, f32[192,768]{1,0:T(8,128)}, f32[192]{0:T(256)}, f32[192]{0:T(256)}, /*index=5*/f32[192]{0...) all-reduce(bf16[192,2304]{0,1:T(8,128)(2,1)S(1)} %copy.328, ...), channel_id=1, replica_groups=mesh['dp'=4,'ctx'=8] {'ctx'}, use_global_device_ids=true, to_apply=%region_33.36 | all-reduce | flops 1771776 | bytes 10635264 | tf_op jit(solution)/shard_map/psum | solution.py:584
  (593 shorter events, 864.7 us)
Async XLA Ops:
  7.2 35.9 %all-gather.9.cloned.1.call-start = ((), (), s32[]{:S(2)}) async-start(), calls=%async_computation.7 | async-start | bytes 4423680 | tf_op jit(solution)/shard_map/all_gather | solution.py:76
  7.9 385.1 %all-reduce.33.cloned.1.call-start = ((), (), s32[]{:S(2)}) async-start(), calls=%async_computation.17 | async-start | bytes 9437184 | tf_op jit(solution)/shard_map/psum | solution.py:12
  49.5 29.0 copy-start.12
  50.2 28.4 copy-start.14
  56.5 913.9 %all-gather.11.cloned.1.call-start = ((), (), s32[]{:S(2)}) async-start(), calls=%async_computation.8 | async-start | bytes 1474560 | tf_op jit(solution)/shard_map/all_gather | solution.py:78
  62.6 18.3 copy-start.70
  66.4 12.0 all-to-all-start
  71.9 905.2 %all-gather.13.cloned.1.call-start = ((), (), s32[]{:S(2)}) async-start(), calls=%async_computation.9 | async-start | bytes 5898240 | tf_op jit(solution)/shard_map/all_gather | solution.py:82
  148.8 10.7 copy-start.67
  148.8 18.1 copy-start.89
  148.8 19.3 copy-start.95
  148.8 19.6 copy-start.96
  148.8 19.8 copy-start.97
  148.8 20.0 copy-start.98
  148.9 20.3 copy-start.99
  148.9 32.0 %copy-start.90 = (bf16[768]{0:T(1024)(128)(2,1)S(1)}, bf16[768]{0:T(1024)(128)(2,1)}, u32[]{:S(2)}) copy-start(bf16[768]{0:T(1024)(128)(2,1)} %param.37) | copy-start | bytes 4612
  148.9 530.6 %all-to-all-start.1 = ((bf16[8,72,64,128]{3,2,1,0:T(8,128)(2,1)}), bf16[8,72,64,128]{3,2,1,0:T(8,128)(2,1)}, u32[]{:S(2)}, u32[]{:S(2)}) async-start(bf16[8,72,64,128]{3,2,1,0:T(8,128)(2,1)} %broadcast_select_fusion.1), calls=%async_computation.1 | async-start | bytes 18874368 | tf_op jit(solution)/shard_map/all_to_all | solution.py:158
  154.1 861.1 %all-gather.15.cloned.1.call-start = ((), (), s32[]{:S(2)}) async-start(), calls=%async_computation.10 | async-start | bytes 5898240 | tf_op jit(solution)/shard_map/all_gather | solution.py:84
  154.7 1846.4 %all-reduce.31.cloned.1.call-start = ((), (), s32[]{:S(2)}) async-start(), calls=%async_computation.16 | async-start | bytes 3145728 | tf_op jit(solution)/shard_map/psum | solution.py:12
  159.5 48.7 %copy-start.91 = (pred[128]{0:T(512)(128)(4,1)}, pred[128]{0:T(512)(128)(4,1)S(1)}, u32[]{:S(2)}) copy-start(pred[128]{0:T(512)(128)(4,1)S(1)} %and_or_fusion.1) | copy-start | bytes 388
  159.7 125.3 %collective-permute-start = (bf16[8,64,1536]{2,1,0:T(8,128)(2,1)}, bf16[8,64,1536]{2,1,0:T(8,128)(2,1)}, u32[]{:S(2)}, u32[]{:S(2)}) collective-permute-start(bf16[8,64,1536]{2,1,0:T(8,128)(2,1)} %get-tuple-element.612), channel_id=1, source_target_pairs={{0,1},{1,2},{2,3},{3,4},{4,5},{5,6},{6,7},{8,9},{9,10},{10,11},{11... | collective-permute-start | bytes 4718600 | tf_op jit(solution)/shard_map/ppermute | solution.py:23
  164.7 123.5 %collective-permute-start.1 = (bf16[8,64,1536]{2,1,0:T(8,128)(2,1)}, bf16[8,64,1536]{2,1,0:T(8,128)(2,1)}, u32[]{:S(2)}, u32[]{:S(2)}) collective-permute-start(bf16[8,64,1536]{2,1,0:T(8,128)(2,1)} %get-tuple-element.613), channel_id=1, source_target_pairs={{1,0},{2,1},{3,2},{4,3},{5,4},{6,5},{7,6},{9,8},{10,9},{11,10},{12... | collective-permute-start | bytes 4718600 | tf_op jit(solution)/shard_map/ppermute | solution.py:25
  181.4 26.7 copy-start.58
  189.0 20.6 copy-start.15
  189.0 22.2 copy-start.13
  209.6 344.9 %copy-start.38 = (pred[8,128,128]{1,2,0:T(8,128)(4,1)}, pred[8,128,128]{1,2,0:T(8,128)(4,1)S(1)}, u32[]{:S(2)}) copy-start(pred[8,128,128]{1,2,0:T(8,128)(4,1)S(1)} %broadcast_compare_fusion) | copy-start | bytes 393220
  411.9 136.2 %copy-start.3 = (f32[8,12,128,128]{2,3,1,0:T(8,128)}, f32[8,12,128,128]{2,3,1,0:T(8,128)S(1)}, u32[]{:S(2)}) copy-start(f32[8,12,128,128]{2,3,1,0:T(8,128)S(1)} %get-tuple-element.625) | copy-start | bytes 18874372
  804.5 18.7 copy-start.52
  804.5 18.7 copy-start.37
  823.2 14.2 copy-start.7
  823.2 14.2 copy-start.49
  823.2 14.2 copy-start.54
  928.7 18.7 copy-start.52
  928.7 18.7 copy-start.37
  947.4 14.2 copy-start.7
  947.4 14.1 copy-start.49
  947.4 14.1 copy-start.54
  961.7 13.2 copy-start.55
  961.8 53.5 %copy-start.8 = (bf16[2,4,128,1536]{2,3,1,0:T(8,128)(2,1)}, bf16[2,4,128,1536]{2,3,1,0:T(8,128)(2,1)S(1)}, u32[]{:S(2)}) copy-start(bf16[2,4,128,1536]{2,3,1,0:T(8,128)(2,1)S(1)} %get-tuple-element.1029) | copy-start | bytes 9437188
  961.8 53.4 %copy-start.50 = (pred[2,4,2,12,8]{4,3,2,1,0:T(8,128)(4,1)}, pred[2,4,2,12,8]{4,3,2,1,0:T(8,128)(4,1)S(1)}, u32[]{:S(2)}) copy-start(pred[2,4,2,12,8]{4,3,2,1,0:T(8,128)(4,1)S(1)} %get-tuple-element.1061) | copy-start | bytes 4612
  975.0 85.5 %copy-start.68 = (f32[1024]{0:T(1024)}, f32[1024]{0:T(1024)S(1)}, u32[]{:S(2)}) copy-start(f32[1024]{0:T(1024)S(1)} %broadcast_multiply_fusion.5) | copy-start | bytes 12292
  977.1 83.4 %copy-start.74 = (f32[1024]{0:T(1024)}, f32[1024]{0:T(1024)S(1)}, u32[]{:S(2)}) copy-start(f32[1024]{0:T(1024)S(1)} %add_rsqrt_fusion.1) | copy-start | bytes 12292
  977.2 38.1 %copy-start.84 = (f32[768]{0:T(1024)S(1)}, f32[768]{0:T(1024)}, u32[]{:S(2)}) copy-start(f32[768]{0:T(1024)} %convert_element_type.231) | copy-start | bytes 9220
  1030.4 19.5 copy-start.32
  1074.5 1479.4 %all-reduce.29.cloned.1.call-start = ((), (), s32[]{:S(2)}) async-start(), calls=%async_computation.15 | async-start | bytes 18874368 | tf_op jit(solution)/shard_map/psum | solution.py:517
  1208.1 21.0 copy-start.2
  1667.0 21.0 copy-start.2
  2057.1 692.5 %reduce-scatter.7.cloned.1.call-start = ((), (), s32[]{:S(2)}) async-start(), calls=%async_computation.11 | async-start | bytes 1474560 | tf_op jit(solution)/shard_map/reduce_scatter | solution.py:553
  2057.8 24.8 copy-start.42
  2057.8 24.8 copy-start.102
  2096.8 463.2 %all-to-all-start.2 = ((bf16[8,72,64,128]{3,2,1,0:T(8,128)(2,1)}), bf16[8,72,64,128]{3,2,1,0:T(8,128)(2,1)}, u32[]{:S(2)}, u32[]{:S(2)}) async-start(bf16[8,72,64,128]{3,2,1,0:T(8,128)(2,1)} %select_convert_fusion), calls=%async_computation.2 | async-start | bytes 18874368 | tf_op jit(solution)/shard_map/all_to_all | solution.py:523
  2102.1 647.5 %reduce-scatter.11.cloned.1.call-start = ((), (), s32[]{:S(2)}) async-start(), calls=%async_computation.13 | async-start | bytes 5898240 | tf_op jit(solution)/shard_map/reduce_scatter | solution.py:571
  2112.1 637.5 %reduce-scatter.9.cloned.1.call-start = ((), (), s32[]{:S(2)}) async-start(), calls=%async_computation.12 | async-start | bytes 5898240 | tf_op jit(solution)/shard_map/reduce_scatter | solution.py:565
  2124.3 660.7 %reduce-scatter.13.cloned.1.call-start = ((), (), s32[]{:S(2)}) async-start(), calls=%async_computation.14 | async-start | bytes 4423680
  2138.7 14.9 copy-start.64
  2143.6 57.8 %collective-permute-start.3 = (bf16[8,64,1536]{2,1,0:T(8,128)(2,1)}, bf16[8,64,1536]{2,1,0:T(8,128)(2,1)}, u32[]{:S(2)}, u32[]{:S(2)}) collective-permute-start(bf16[8,64,1536]{2,1,0:T(8,128)(2,1)} %copy.305), channel_id=1, source_target_pairs={{1,0},{2,1},{3,2},{4,3},{5,4},{6,5},{7,6},{9,8},{10,9},{11,10},{12... | collective-permute-start | bytes 4718600 | tf_op jit(solution)/shard_map/ppermute | solution.py:25
  2147.3 66.5 %collective-permute-start.2 = (bf16[8,64,1536]{2,1,0:T(8,128)(2,1)}, bf16[8,64,1536]{2,1,0:T(8,128)(2,1)}, u32[]{:S(2)}, u32[]{:S(2)}) collective-permute-start(bf16[8,64,1536]{2,1,0:T(8,128)(2,1)} %copy.304), channel_id=1, source_target_pairs={{0,1},{1,2},{2,3},{3,4},{4,5},{5,6},{6,7},{8,9},{9,10},{10,11},{11... | collective-permute-start | bytes 4718600 | tf_op jit(solution)/shard_map/ppermute | solution.py:23
  2213.7 10.8 slice-start
  2236.5 317.5 %copy-start.34 = (f32[8,128,768]{1,2,0:T(8,128)S(1)}, f32[8,128,768]{1,2,0:T(8,128)}, u32[]{:S(2)}) copy-start(f32[8,128,768]{1,2,0:T(8,128)} %reshape.483) | copy-start | bytes 9437188
  2236.5 317.5 %copy-start.92 = (pred[128]{0:T(512)(128)(4,1)S(1)}, pred[128]{0:T(512)(128)(4,1)}, u32[]{:S(2)}) copy-start(pred[128]{0:T(512)(128)(4,1)} %copy-done.91) | copy-start | bytes 388
  2745.3 19.7 copy-start.10
  2745.4 19.7 copy-start.60
  2745.4 19.7 copy-start.62
  2745.4 19.7 copy-start.66
  (78 other events, 391.8 us)
Sparse Core Ops, SparseCore 0:
  9.6 33.4 all-gather.8
  56.6 336.3 all-reduce.32
  394.6 16.3 all-gather.10
  412.4 37.4 all-gather.12
  451.3 37.4 all-gather.14
  1074.7 88.0 all-reduce.30
  2057.2 496.6 all-reduce.28
  2557.1 24.6 reduce-scatter.6
  2584.5 47.8 reduce-scatter.10
  2634.8 47.8 reduce-scatter.8
  2745.5 39.4 reduce-scatter.12
where the time goes:
time: 3110 us; the launch traced here: 3100 us
  local copies, waits for them, and re-layouts  1230 us (40%)
  blocking collectives  617 us (20%)
  waiting for transfers between devices  550 us (18%)
  other arithmetic  331 us (11%)
  matrix products  314 us (10%)
    psum x1, waiting for transfers between devices, body(): global_sum, query_sum = lax.psum((global_grad, global_q_part), 'ctx')  306 us
    psum x1, blocking collectives, body(): lax.psum((shares[0], shares[1], shares[2], shares[3], shares[4], shares[5...  301 us
    all_gather x2, blocking collectives, combined_all(): pieces = jax.tree.map(lambda part: lax.all_gather(part, axis), value)  132 us
    transpose x9, local copies, waits for them, and re-layouts, slab_view(): parted.transpose(perm_axes)  120 us
    psum x1, blocking collectives, body(): lax.psum(partial_mix, 'ctx').astype(jnp.bfloat16)  115 us
    slice x2, local copies, waits for them, and re-layouts, attend_backward(): grad_slabs[:, :, :, 0]  106 us
    psum x2, waiting for transfers between devices, spread_2(): return lax.psum(kept, axis)  91.5 us
    scatter-add x1, other arithmetic, body(): jax.ops.segment_sum(returned.reshape((-1,) + slab_shape), received.reshap...  91.1 us
  transfers between devices with their start and end apart: 18, of which 8 were waited for; matrix products, arithmetic and copies ran while one was open for 57% of the time, Pallas kernels for 0%

commit v1 on v0

v1 whole, which is shorter than its diff:
```python
import jax
import jax.numpy as jnp
from jax import lax
from jax.experimental import pallas as pl
from jax.experimental.pallas import tpu as pltpu
from jax.sharding import PartitionSpec as P

f32, bf16 = jnp.float32, jnp.bfloat16
eps_norm = 1e-12
far = 1e30
doc_min = 200
lanes_n = 128
vmem_cap = 56 * 2**20


def swap_pieces(pieces, axis, stride):
    count, size = pieces.shape[0], lax.axis_size(axis)
    groups = None
    if count < size:
        span = stride * count
        starts = [base + offset for base in range(0, size, span) for offset in range(stride)]
        groups = [[start + i * stride for i in range(count)] for start in starts]
    return lax.all_to_all(pieces, axis, 0, 0, axis_index_groups=groups, tiled=True)


def share_pieces(piece, axis, stride, count):
    size = lax.axis_size(axis)
    member = (lax.axis_index(axis) // stride) % count
    came = [piece]
    for k in range(1, count):
        pairs = [(i, ((i // stride % count) ^ k) * stride + i % stride + i // (stride * count) * (stride * count)) for i in range(size)]
        came.append(lax.ppermute(piece, axis, pairs))
    came = jnp.stack(came)
    return jnp.stack([lax.dynamic_index_in_dim(came, member ^ i, 0, keepdims=False) for i in range(count)])


def sum_pieces(pieces, axis, stride):
    count = pieces.shape[0]
    size = lax.axis_size(axis)
    member = (lax.axis_index(axis) // stride) % count
    total = lax.dynamic_index_in_dim(pieces, member, 0, keepdims=False).astype(f32)
    for k in range(1, count):
        pairs = [(i, ((i // stride % count) ^ k) * stride + i % stride + i // (stride * count) * (stride * count)) for i in range(size)]
        out = lax.dynamic_index_in_dim(pieces, member ^ k, 0, keepdims=False)
        total = total + lax.ppermute(out.astype(bf16), axis, pairs).astype(f32)
    return total


def stages_of(size):
    stages, stride = [], 1
    while stride < size:
        count = 2 if stride == 1 else min(4, size // stride)
        stages.append((stride, count))
        stride *= count
    return stages


def cut(value, dim, count):
    rows, cols = value.shape
    if dim == 0:
        return value.reshape(count, rows // count, cols)
    return jnp.stack([value[:, i * (cols // count) : (i + 1) * (cols // count)] for i in range(count)])


def joined(pieces, dim):
    return jnp.concatenate([pieces[i] for i in range(pieces.shape[0])], axis=dim)


def reduce_dp(grad):
    count = grad.shape[0]
    total, stride = grad, 1
    while stride < count:
        half = total.reshape(total.shape[0] // 2, 2, *grad.shape[1:]).transpose(1, 0, 2, 3)
        total = sum_pieces(half, "dp", stride).astype(bf16)
        stride *= 2
    return total[0]


def reduce_ctx(grad):
    stages = stages_of(lax.axis_size("ctx"))
    total = grad
    for place, (stride, count) in enumerate(stages):
        total = sum_pieces(cut(total, (place + 1) % 2, count), "ctx", stride).astype(bf16)
    for place, (stride, count) in reversed(list(enumerate(stages))):
        total = joined(share_pieces(total, "ctx", stride, count), (place + 1) % 2)
    return total


def reduce_all(grad):
    return reduce_ctx(reduce_dp(grad))


def mask_features(seg, rand, block):
    tokens = seg.shape[0]
    blocks, heads = rand.shape[:2]
    seg_limit = tokens // doc_min + 1
    used = seg_limit + 2 * blocks
    width = -(-used // lanes_n) * lanes_n
    ids = jnp.arange(blocks, dtype=jnp.int32)

    def hot(values):
        return (values[..., None] == ids).astype(jnp.int32)

    near = hot(ids - 1) + hot(ids) + hot(ids + 1) + hot(ids * 0) + hot(ids * 0 + blocks - 1)
    counts = near[:, None, :] + jnp.sum(hot(rand), axis=2)
    edge = (ids == 0) | (ids == blocks - 1)
    counts = jnp.where(edge[:, None, None], 1, counts).transpose(1, 2, 0)
    log_count = jnp.log(jnp.maximum(counts, 1).astype(f32))
    high = log_count.astype(bf16).astype(f32)
    low = jnp.where(counts > 0, log_count - high, 0.0)
    high = jnp.where(counts > 0, high, -far)
    table = jnp.concatenate(
        [
            jnp.zeros((heads, blocks, seg_limit), f32),
            high,
            low,
            jnp.zeros((heads, blocks, width - used), f32),
        ],
        axis=2,
    )
    lane = jnp.arange(width, dtype=jnp.int32)[None]
    own = (jnp.arange(tokens, dtype=jnp.int32) // block)[:, None]
    is_seg = lane < seg_limit
    same = lane == seg[:, None]
    key_feat = jnp.where(is_seg & same, 1.0, 0.0).astype(bf16)
    own_lane = (lane - seg_limit == own) | (lane - seg_limit - blocks == own)
    query_feat = jnp.where(
        is_seg, jnp.where(same, 0.0, -far), jnp.where(own_lane, 1.0, 0.0)
    ).astype(bf16)
    return key_feat, query_feat, table


def fill_keys(k_ref, key_feat_ref, table_ref, keys):
    tokens, width = key_feat_ref.shape
    blocks = table_ref.shape[1]
    feat = key_feat_ref[...].astype(f32).reshape(blocks, tokens // blocks, width) + table_ref[0][:, None, :]
    keys[:, :lanes_n] = k_ref[...]
    keys[:, lanes_n:] = feat.reshape(tokens, width).astype(bf16)


def forward_kernel(
    q_ref, k_ref, v_ref, key_feat_ref, query_feat_ref, table_ref, out_ref, keys, vals, *, half, tile
):
    side = pl.program_id(1)
    tokens = q_ref.shape[0]
    fill_keys(k_ref, key_feat_ref, table_ref, keys)
    vals[:, :lanes_n] = v_ref[...]
    vals[:, lanes_n:] = jnp.ones((tokens, lanes_n), bf16)

    @pl.loop(0, tokens // tile)
    def _(step):
        rows = pl.ds(pl.multiple_of(step * tile, tile), tile)
        keep = lax.broadcasted_iota(jnp.int32, (tile, lanes_n), 1) // half == side
        q = jnp.where(keep, q_ref[rows, :] * bf16(half**-0.5), bf16(0))
        q = jnp.concatenate([q, query_feat_ref[rows, :]], axis=1)
        scores = lax.dot_general(
            q, keys[...], (((1,), (1,)), ((), ())), preferred_element_type=f32
        )
        top = jnp.max(scores, axis=1, keepdims=True)
        weights = jnp.exp(scores - top).astype(bf16)
        mixed = jnp.dot(weights, vals[...], preferred_element_type=f32)
        out = (mixed[:, :lanes_n] / mixed[:, lanes_n:]).astype(bf16)
        other = jnp.where(side == 0, jnp.zeros_like(out), out_ref[rows, :])
        out_ref[rows, :] = jnp.where(keep, out, other)


def backward_kernel(
    q_ref,
    k_ref,
    v_ref,
    grad_ref,
    key_feat_ref,
    query_feat_ref,
    table_ref,
    dq_ref,
    dk_ref,
    dv_ref,
    keys,
    dk_sum,
    dv_sum,
    *,
    half,
    tile,
):
    side = pl.program_id(1)
    tokens = q_ref.shape[0]
    fill_keys(k_ref, key_feat_ref, table_ref, keys)

    @pl.when(side == 0)
    def _():
        dk_sum[...] = jnp.zeros_like(dk_sum)
        dv_sum[...] = jnp.zeros_like(dv_sum)
        dq_ref[...] = jnp.zeros_like(dq_ref)

    @pl.loop(0, tokens // tile)
    def _(step):
        rows = pl.ds(pl.multiple_of(step * tile, tile), tile)
        keep = lax.broadcasted_iota(jnp.int32, (tile, lanes_n), 1) // half == side
        q = jnp.where(keep, q_ref[rows, :] * bf16(half**-0.5), bf16(0))
        grad = jnp.where(keep, grad_ref[rows, :], bf16(0))
        q_wide = jnp.concatenate([q, query_feat_ref[rows, :]], axis=1)
        scores = lax.dot_general(
            keys[...], q_wide, (((1,), (1,)), ((), ())), preferred_element_type=f32
        )
        raw = jnp.exp(scores - jnp.max(scores, axis=0, keepdims=True))
        probs = raw * (1.0 / jnp.sum(raw, axis=0, keepdims=True))
        dprobs = lax.dot_general(
            v_ref[...], grad, (((1,), (1,)), ((), ())), preferred_element_type=f32
        )
        inner = jnp.sum(probs * dprobs, axis=0, keepdims=True)
        dscores = (probs * (dprobs - inner)).astype(bf16)
        dv_sum[...] += jnp.dot(probs.astype(bf16), grad, preferred_element_type=f32)
        dk_sum[...] += jnp.dot(dscores, q, preferred_element_type=f32)
        dq = lax.dot_general(
            dscores, k_ref[...], (((0,), (0,)), ((), ())), preferred_element_type=f32
        )
        dq_ref[rows, :] += jnp.where(keep, (dq * half**-0.5).astype(bf16), bf16(0))

    @pl.when(side == 1)
    def _():
        dk_ref[...] = dk_sum[...].astype(bf16)
        dv_ref[...] = dv_sum[...].astype(bf16)


def attend(kernel, arrays, features, outs, scratch_n, half, name, after=(), first=0, count=None):
    tokens, width = arrays[0].shape
    key_feat, query_feat, table = features
    count = width // lanes_n if count is None else count
    feat_width = key_feat.shape[1]
    tile = 256 if tokens <= 2048 else 128
    pair = pl.BlockSpec((tokens, lanes_n), lambda p, s: (0, p + first))
    pair_out = pl.BlockSpec((tokens, lanes_n), lambda p, s: (0, p))
    whole = pl.BlockSpec((tokens, feat_width), lambda p, s: (0, 0), pipeline_mode=pl.Buffered(1))
    shape = jax.ShapeDtypeStruct((tokens, count * lanes_n), bf16)
    scratch = [pltpu.VMEM((tokens, lanes_n + feat_width), bf16)]
    if scratch_n == 1:
        scratch = scratch + [pltpu.VMEM((tokens, 2 * lanes_n), bf16)]
    else:
        scratch = scratch + [pltpu.VMEM((tokens, lanes_n), f32)] * 2
    work = count * lanes_n // half * tokens * tokens

    def run(*refs):
        held = len(arrays) + 3
        kernel(*refs[:held], *refs[held + len(after) :], half=half, tile=tile)

    return pl.pallas_call(
        run,
        grid=(count, 2),
        in_specs=[pair] * len(arrays)
        + [whole, whole]
        + [pl.BlockSpec((1,) + table.shape[1:], lambda p, s: (2 * (p + first) + s, 0, 0))]
        + [pl.BlockSpec(memory_space=pl.ANY)] * len(after),
        out_specs=[pair_out] * outs,
        out_shape=[shape] * outs,
        scratch_shapes=scratch,
        compiler_params=pltpu.CompilerParams(vmem_limit_bytes=vmem_cap),
        cost_estimate=pl.CostEstimate(
            flops=work * 1024 * (1 if outs == 1 else 2),
            bytes_accessed=tokens * width * 2 * (len(arrays) + outs),
            transcendentals=work,
        ),
        name=name,
    )(*arrays, key_feat, query_feat, table, *after)


def pack_kernel(weight_ref, *refs):
    out_ref = refs[-1]
    rows = weight_ref.shape[0]
    out_ref[:rows, :] = weight_ref[...]
    out_ref[rows:, :] = jnp.zeros_like(out_ref[rows:, :])
    for place, ref in enumerate(refs[:-1]):
        out_ref[rows + place : rows + place + 1, : ref.shape[1]] = ref[...]


def pack_weights(weight, vectors):
    rows, cols = weight.shape
    extra = -(-len(vectors) // 16) * 16
    return pl.pallas_call(
        pack_kernel,
        out_shape=jax.ShapeDtypeStruct((rows + extra, cols), weight.dtype),
        name="pack_weights",
    )(weight, *[v[None] for v in vectors])


def norm_forward(values_in, gain_vec, offset_vec):
    centred = values_in - jnp.mean(values_in, axis=-1, keepdims=True)
    inverse = lax.rsqrt(jnp.mean(centred * centred, axis=-1, keepdims=True) + eps_norm)
    normed = centred * inverse
    return (normed * gain_vec + offset_vec, normed, inverse)


def norm_backward(incoming, normed, inverse, gain_vec):
    scaled = incoming * gain_vec
    centred_grad = (
        scaled
        - jnp.mean(scaled, axis=-1, keepdims=True)
        - normed * jnp.mean(scaled * normed, axis=-1, keepdims=True)
    )
    return (centred_grad * inverse, jnp.sum(incoming * normed, axis=0), jnp.sum(incoming, axis=0))


def body(
    inputs,
    segments,
    random_blocks,
    cotangent,
    qkv_weight,
    qv_bias,
    out_weight,
    out_bias,
    norm1_gain,
    norm1_bias,
    up_weight,
    up_bias,
    down_weight,
    down_bias,
    norm2_gain,
    norm2_bias,
):
    seq_count, run, width = inputs.shape
    per_dev, head_count, rand_count = random_blocks.shape[1:]
    block = run // per_dev
    head_size = width // head_count
    dp_count = lax.axis_size("dp")
    ctx_count = lax.axis_size("ctx")
    ctx_index = lax.axis_index("ctx")
    team = ctx_count // seq_count
    tokens = seq_count * run

    x = swap_pieces(inputs, "ctx", team).reshape(tokens, width)
    lists = swap_pieces(random_blocks.reshape(seq_count, 1, -1), "ctx", team)
    grad_result = swap_pieces(cotangent, "ctx", team).reshape(tokens, width)

    def back_to_runs(rows):
        return swap_pieces(rows.reshape(seq_count, run, width), "ctx", team)

    vectors = (qv_bias, out_bias, norm1_gain, norm1_bias, up_bias, down_bias, norm2_gain, norm2_bias)
    sizes = [v.shape[0] for v in vectors]
    qkv_rows, qkv_cols = qkv_weight.shape
    first = lax.all_gather(pack_weights(qkv_weight, vectors), "dp", axis=0)
    weight_qkv = first[:, :qkv_rows].reshape(-1, qkv_cols)
    split = [
        first[:, qkv_rows + place, :size].reshape(-1).astype(f32) for place, size in enumerate(sizes)
    ]
    bias_qv, bias_out, gain_one, shift_one, bias_up, bias_down, gain_two, shift_two = split
    weight_out = lax.all_gather(out_weight, "dp", axis=0, tiled=True)
    weight_up = lax.all_gather(up_weight, "dp", axis=0, tiled=True)
    weight_down = lax.all_gather(down_weight, "dp", axis=0, tiled=True)

    seq_index = ctx_index // team
    seg = lax.dynamic_index_in_dim(segments, seq_index, 0, keepdims=False)
    lists = lists.reshape(seq_count, per_dev, head_count, rand_count)
    if team > 1:
        team_index = ctx_index % team
        held = -(-head_count // (2 * team)) * 2
        spare = held * team - head_count
        lists = share_pieces(lists, "ctx", 1, team).transpose(1, 0, 2, 3, 4)
        lists = jnp.pad(lists.reshape(-1, head_count, rand_count), ((0, 0), (0, spare), (0, 0)))
        lists = lax.dynamic_slice_in_dim(lists, team_index * held, held, 1)
    else:
        lists = lists.reshape(-1, head_count, rand_count)
    features = mask_features(seg, lists, block)

    def to_heads(rows):
        if team == 1:
            return rows
        rows = jnp.pad(rows, ((0, 0), (0, spare * head_size)))
        part = swap_pieces(rows.reshape(tokens, team, -1).transpose(1, 0, 2), "ctx", 1)
        part = part.reshape(team, seq_count, run, -1).transpose(1, 0, 2, 3)
        return part.reshape(team * tokens, -1)

    def to_tokens(part):
        if team == 1:
            return part
        part = part.reshape(seq_count, team, run, -1).transpose(1, 0, 2, 3)
        rows = swap_pieces(part.reshape(team, tokens, -1), "ctx", 1)
        return rows.transpose(1, 0, 2).reshape(tokens, -1)[:, :width]

    projected = jnp.dot(x, weight_qkv, preferred_element_type=f32)
    queries = (projected[:, :width] + bias_qv[:width]).astype(bf16)
    keys = projected[:, width : 2 * width].astype(bf16)
    values = (projected[:, 2 * width :] + bias_qv[width:]).astype(bf16)
    heads = tuple(to_heads(part) for part in (queries, keys, values))
    attended = attend(forward_kernel, heads, features, 1, 1, head_size, "attend_forward")[0]
    attended = to_tokens(attended)
    branch = jnp.dot(attended, weight_out, preferred_element_type=f32) + bias_out
    hidden, normed_one, inverse_one = norm_forward(x.astype(f32) + branch, gain_one, shift_one)
    hidden_low = hidden.astype(bf16)
    upper = jnp.dot(hidden_low, weight_up, preferred_element_type=f32) + bias_up
    cdf = 0.5 * (1.0 + lax.erf(upper * 0.5**0.5))
    active = (upper * cdf).astype(bf16)
    slope = (cdf + upper * jnp.exp(-0.5 * upper * upper) * (2.0 * jnp.pi) ** -0.5).astype(bf16)
    mlp_out = jnp.dot(active, weight_down, preferred_element_type=f32) + bias_down
    result, normed_two, inverse_two = norm_forward(hidden + mlp_out, gain_two, shift_two)
    layer_out = back_to_runs(result.astype(bf16))

    grad_sum, grad_gain_two, grad_shift_two = norm_backward(
        grad_result.astype(f32), normed_two, inverse_two, gain_two
    )
    grad_mlp = grad_sum.astype(bf16)

    def weight_grad(left, right):
        grad = lax.dot_general(left, right, (((0,), (0,)), ((), ())), preferred_element_type=f32)
        return grad.astype(bf16).reshape(dp_count, -1, grad.shape[1])

    down_total = reduce_all(weight_grad(active, grad_mlp))
    grad_down_b = jnp.sum(grad_mlp, axis=0, dtype=f32)
    grad_active = lax.dot_general(
        grad_mlp, weight_down, (((1,), (1,)), ((), ())), preferred_element_type=f32
    )
    grad_upper = (grad_active * slope.astype(f32)).astype(bf16)
    up_total = reduce_all(weight_grad(hidden_low, grad_upper))
    grad_up_b = jnp.sum(grad_upper, axis=0, dtype=f32)
    grad_hidden = grad_sum + lax.dot_general(
        grad_upper, weight_up, (((1,), (1,)), ((), ())), preferred_element_type=f32
    )
    grad_pre, grad_gain_one, grad_shift_one = norm_backward(
        grad_hidden, normed_one, inverse_one, gain_one
    )
    grad_branch = grad_pre.astype(bf16)
    out_total = reduce_all(weight_grad(attended, grad_branch))
    grad_out_b = jnp.sum(grad_branch, axis=0, dtype=f32)
    grad_att = lax.dot_general(
        grad_branch, weight_out, (((1,), (1,)), ((), ())), preferred_element_type=f32
    ).astype(bf16)
    back = attend(
        backward_kernel, heads + (to_heads(grad_att),), features, 3, 2, head_size, "attend_backward"
    )
    grad_proj = jnp.concatenate([to_tokens(part) for part in back], axis=1)
    grad_input = grad_pre + lax.dot_general(
        grad_proj, weight_qkv, (((1,), (1,)), ((), ())), preferred_element_type=f32
    )
    input_grad = back_to_runs(grad_input.astype(bf16))
    grad_qkv_b = jnp.sum(grad_proj, axis=0, dtype=f32)
    grad_qv_b = jnp.concatenate([grad_qkv_b[:width], grad_qkv_b[2 * width :]])
    grad_vecs = (
        grad_qv_b,
        grad_out_b,
        grad_gain_one,
        grad_shift_one,
        grad_up_b,
        grad_down_b,
        grad_gain_two,
        grad_shift_two,
    )
    per_row = -(-sum(sizes) // qkv_rows)
    side = jnp.concatenate([v.astype(bf16).reshape(dp_count, -1) for v in grad_vecs], axis=1)
    side = jnp.pad(side, ((0, 0), (0, per_row * qkv_rows - sum(sizes))))
    side = side.reshape(dp_count, qkv_rows, per_row)
    side_cols = -(-per_row // (2 * lanes_n)) * 2 * lanes_n
    side = jnp.pad(side, ((0, 0), (0, 0), (0, side_cols - per_row)))
    last = jnp.concatenate([weight_grad(x, grad_proj), side], axis=2)
    last_total = reduce_all(last).astype(f32)
    qkv_total = last_total[:, :qkv_cols]
    flat_total = last_total[:, qkv_cols : qkv_cols + per_row].reshape(-1)
    vec_totals, start = [], 0
    for size in sizes:
        vec_totals.append(flat_total[start : start + size])
        start += size
    return (
        layer_out,
        input_grad,
        qkv_total,
        vec_totals[0],
        out_total.astype(f32),
        vec_totals[1],
        vec_totals[2],
        vec_totals[3],
        up_total.astype(f32),
        vec_totals[4],
        down_total.astype(f32),
        vec_totals[5],
        vec_totals[6],
        vec_totals[7],
    )


def solution(mesh):
    tokens = P("dp", "ctx", None)
    matrix, vector = P("dp", None), P("dp")
    weights = (matrix, vector, matrix, vector, vector, vector, matrix, vector, matrix, vector, vector, vector)
    return jax.shard_map(
        body,
        mesh=mesh,
        in_specs=(tokens, matrix, P("dp", "ctx", None, None), tokens) + weights,
        out_specs=(tokens, tokens) + weights,
        check_vma=False,
    )
```

time: 3110 us -> 608 us (0.20)
  local copies, waits for them, and re-layouts: 1230 us -> 66.2 us
  blocking collectives: 617 us -> 51.8 us
  waiting for transfers between devices: 550 us -> 139 us
  other arithmetic: 331 us -> 55 us
  matrix products: 314 us -> 88.2 us
  Pallas kernels: 0 us -> 123 us
  starting transfers between devices: 30 us -> 63.2 us
    psum x3 -> x0, blocking collectives: 451 us -> none  [the longest x1 301 us: body(): lax.psum((shares[0], shares[1], shares[2], shares[3], shares[4], shares[5...]
    psum x3 -> x0, waiting for transfers between devices: 398 us -> none  [the longest x1 306 us: body(): global_sum, query_sum = lax.psum((global_grad, global_q_part), 'ctx')]
    reshape x33 -> x7, local copies, waits for them, and re-layouts: 316 us -> 5.88 us  [the longest x4 3.94 us: body(): v.astype(bf16).reshape(dp_count, -1)]
    dot_general x32 -> x12, matrix products: 314 us -> 88.2 us  [the longest x4 22.3 us: weight_grad(): lax.dot_general(left, right, (((0,), (0,)), ((), ())), preferred_element_...]
    slice x21 -> x17, local copies, waits for them, and re-layouts: 190 us -> 19.1 us  [the longest x8 6.68 us: body(): vec_totals.append(flat_total[start:start + size])]
    transpose x12 -> x0, local copies, waits for them, and re-layouts: 149 us -> none  [the longest x9 120 us: slab_view(): parted.transpose(perm_axes)]
    all_gather x4 -> x0, blocking collectives: 144 us -> none  [the longest x2 132 us: combined_all(): pieces = jax.tree.map(lambda part: lax.all_gather(part, axis), value)]
    pallas_call x0 -> x3, Pallas kernels: none -> 123 us  [the longest x2 121 us: attend(): pl.pallas_call(run, grid=(count, 2), in_specs=[pair] * len(arrays) + [who...]
  transfers between devices with their start and end apart: 18 -> 47, of which waited for: 8 -> 15; matrix products, arithmetic and copies ran while one was open for 57% -> 22% of each run, Pallas kernels for 0% -> 8%
where the time goes in v1:
time: 608 us; the launch traced here: 601 us
  waiting for transfers between devices  139 us (23%)
  Pallas kernels  123 us (20%)
  matrix products  88.2 us (15%)
  local copies, waits for them, and re-layouts  66.2 us (11%)
  starting transfers between devices  63.2 us (10%)
  other arithmetic  55 us (9%)
  blocking collectives  51.8 us (9%)
  between operations  15 us (2%)
    pallas_call x2, Pallas kernels, attend(): pl.pallas_call(run, grid=(count, 2), in_specs=[pair] * len(arrays) + [who...  121 us
    ppermute x16, waiting for transfers between devices, share_pieces(): came.append(lax.ppermute(piece, axis, pairs))  63.9 us
    all_to_all x2, blocking collectives, swap_pieces(): lax.all_to_all(pieces, axis, 0, 0, axis_index_groups=groups, tiled=True)  51.8 us
    all_to_all x3, waiting for transfers between devices, swap_pieces(): lax.all_to_all(pieces, axis, 0, 0, axis_index_groups=groups, tiled=True)  39.4 us
    ppermute x24, waiting for transfers between devices, sum_pieces(): total = total + lax.ppermute(out.astype(bf16), axis, pairs).astype(f32)  33.3 us
    ppermute x16, starting transfers between devices, share_pieces(): came.append(lax.ppermute(piece, axis, pairs))  26.1 us
    ppermute x24, starting transfers between devices, sum_pieces(): total = total + lax.ppermute(out.astype(bf16), axis, pairs).astype(f32)  24.5 us
    dot_general x4, matrix products, weight_grad(): lax.dot_general(left, right, (((0,), (0,)), ((), ())), preferred_element_...  22.3 us
  transfers between devices with their start and end apart: 47, of which 15 were waited for; matrix products, arithmetic and copies ran while one was open for 22% of the time, Pallas kernels for 8%

profile of v1, /device:TPU:0, one launch (start us, length us, event | category | flops | bytes accessed | tf_op | source)
XLA Modules:
  0.0 601.3 jit_solution(10964631065534285501)
XLA Ops:
  17.2 2.3 pack_weights.1
  21.2 13.5 %all_to_all.25 = s32[8,1,72]{2,1,0:T(1,128)S(1)} all-to-all(s32[8,1,72]{2,1,0:T(1,128)S(1)} %copy.39), channel_id=1, replica_groups=mesh['dp'=4,'ctx'=8] {'ctx'}, dimensions={0} | all-to-all | bytes 4608 | tf_op jit(solution)/shard_map/all_to_all | solution.py:23
  34.7 38.3 %all_to_all.26 = bf16[8,128,768]{2,1,0:T(8,128)(2,1)S(1)} all-to-all(bf16[8,128,768]{2,1,0:T(8,128)(2,1)S(1)} %copy-done.12), channel_id=1, replica_groups=mesh['dp'=4,'ctx'=8] {'ctx'}, dimensions={0} | all-to-all | bytes 3145728 | tf_op jit(solution)/shard_map/all_to_all | solution.py:23
  73.0 3.6 all-to-all-start
  82.2 4.4 slice.206
  87.3 25.8 %all-to-all-done = bf16[8,128,768]{2,1,0:T(8,128)(2,1)S(1)} async-done(((bf16[8,128,768]{2,1,0:T(8,128)(2,1)}), bf16[8,128,768]{2,1,0:T(8,128)(2,1)S(1)}, u32[]{:S(2)}, u32[]{:S(2)}) %all-to-all-start) | async-done | bytes 1572896 | tf_op jit(solution)/shard_map/all_to_all | solution.py:23
  113.1 8.8 %convolution_bitcast_fusion = f32[1024,2304]{1,0:T(8,128)} fusion(bf16[1024,768]{1,0:T(8,128)(2,1)S(1)} %bitcast.285, bf16[768,2304]{1,0:T(8,128)(2,1)} %bitcast.273), kind=kOutput, calls=%fused_computation.9 | convolution fusion | flops 3623878656 | bytes 14548992 | tf_op jit(solution)/shard_map/dot_general | solution.py:379
  121.9 3.6 slice.268.refs_1_
  127.4 5.1 fusion.8
  132.5 46.6 %attend_forward.1 = bf16[1024,768]{1,0:T(8,128)(2,1)} custom-call(bf16[1024,768]{1,0:T(8,128)(2,1)} %get-tuple-element.39.refs_0_, bf16[1024,768]{1,0:T(8,128)(2,1)} %slice.268.refs_1_, bf16[1024,768]{1,0:T(8,128)(2,1)} %get-tuple-element.38.refs_2_, bf16[1024,128]{1,0:T(8,128)(2,1)} %get-tuple-element.104.refs_3_.refs_4_, ...), custom_call_target="tpu_custom_call" | custom-call | flops 12884901888 | bytes 6291456 | tf_op jit(solution)/shard_map/attend_forward/pallas_call | solution.py:246
  179.1 4.8 fusion.102
  183.9 2.4 multiply_reduce_fusion.3
  187.1 12.4 %multiply_convert_fusion.1 = (bf16[1024,3072]{1,0:T(8,128)(2,1)}, f32[1024,3072]{1,0:T(8,128)}) fusion(f32[3072]{0:T(1024)S(1)} %bitcast.314, bf16[768,3072]{1,0:T(8,128)(2,1)} %all-gather.8.cloned.1.call-done, f32[1024,768]{1,0:T(8,128)} %get-tuple-element.106, f32[768]{0:T(1024)S(1)} %reshape.417, f32[768]{0:T(1024)S(1)} %reshape.416, ...), kind=kOutput, calls=%fused_computation.7 | convolution fusion | flops 4854644736 | bytes 26765312 | tf_op jit(solution)/shard_map/dot_general | solution.py:389
  199.5 9.3 %fusion.103 = (f32[1024]{0:T(1024)S(1)}, f32[1024,768]{1,0:T(8,128)S(1)}) fusion(f32[768]{0:T(1024)S(1)} %reshape.419, bf16[1024,3072]{1,0:T(8,128)(2,1)} %get-tuple-element.107, bf16[3072,768]{1,0:T(8,128)(2,1)} %all-gather.10.cloned.1.call-done, f32[768]{0:T(1024)S(1)} %reshape.417, f32[768]{0:T(1024)S(1)} %reshape.416, f32[1024]{0:T(1024)S(1)} %add_rsqrt_fusion.1, ...), kind=kOutput, calls=%fused_computation.296 | convolution fusion | flops 4837342208 | bytes 17323008 | tf_op jit(solution)/shard_map/dot_general | solution.py:393
  209.4 3.4 fusion.16
  212.8 1.8 convert_reduce_fusion.2
  214.6 7.5 %convolution_convert_fusion = bf16[3072,768]{1,0:T(8,128)(2,1)} fusion(bf16[1024,3072]{1,0:T(8,128)(2,1)S(1)} %bitcast.321, f32[1024,768]{1,0:T(8,128)S(1)} %get-tuple-element.35), kind=kOutput, calls=%fused_computation.12 | convolution fusion | flops 4834983936 | bytes 14155776 | tf_op jit(solution)/shard_map/dot_general | solution.py:403
  222.1 12.4 %fusion.104 = (bf16[3072]{0:T(1024)(128)(2,1)}, bf16[1024,3072]{1,0:T(8,128)(2,1)S(1)}) fusion(f32[1024,3072]{1,0:T(8,128)} %get-tuple-element.108, f32[3072]{0:T(1024)S(1)} %bitcast.315, bf16[3072,768]{1,0:T(8,128)(2,1)S(1)} %bitcast.319, f32[1024,768]{1,0:T(8,128)S(1)} %get-tuple-element.35), kind=kOutput, calls=%fused_computation.297 | convolution fusion | flops 4876661760 | bytes 26757120 | tf_op jit(solution)/shard_map/dot_general | solution.py:408
  234.5 10.7 %multiply_reduce_fusion = (bf16[768]{0:T(1024)(128)(2,1)}, f32[1024]{0:T(1024)S(1)}, f32[1024]{0:T(1024)S(1)}, bf16[768]{0:T(1024)(128)(2,1)}, f32[1024,768]{1,0:T(8,128)S(1)}) fusion(f32[1024,768]{1,0:T(8,128)} %get-tuple-element.106, f32[1024]{0:T(1024)S(1)} %add_rsqrt_fusion.1, f32[1024]{0:T(1024)S(1)} %broadcast_multiply_fusion.4, ...), kind=kOutput, calls=%fused_computation.38 | convolution fusion | flops 4839698432 | bytes 20469760 | tf_op jit(solution)/shard_map/dot_general | solution.py:414
  245.2 3.3 convert_reduce_fusion.1
  250.0 2.6 convolution_convert_fusion.3.refs_3_
  252.5 74.5 %attend_backward.1 = (bf16[1024,768]{1,0:T(8,128)(2,1)}, bf16[1024,768]{1,0:T(8,128)(2,1)}, bf16[1024,768]{1,0:T(8,128)(2,1)}) custom-call(bf16[1024,768]{1,0:T(8,128)(2,1)} %get-tuple-element.39.refs_0_, bf16[1024,768]{1,0:T(8,128)(2,1)} %slice.268.refs_1_, bf16[1024,768]{1,0:T(8,128)(2,1)} %get-tuple-element.38.refs_2_, ...), custom_call_target="tpu_custom_call" | custom-call | flops 25769803776 | bytes 11010048 | tf_op jit(solution)/shard_map/attend_backward/pallas_call | solution.py:246
  327.0 1.7 constant_dynamic-update-slice_fusion.2
  331.0 5.0 add_convert_fusion
  338.4 4.5 convolution_convert_fusion.2
  342.8 3.0 reduce.6
  345.9 3.3 dynamic-slice_bitcast_fusion
  365.8 1.8 reshape.410
  371.2 2.1 collective-permute-start.14
  373.2 2.3 collective-permute-start.15
  377.0 4.3 all-to-all-start.4
  382.2 2.0 collective-permute-start.16
  384.1 2.4 collective-permute-start.17
  386.6 9.0 %convolution_convert_fusion.1 = bf16[768,3072]{1,0:T(8,128)(2,1)S(1)} fusion(bf16[1024,3072]{1,0:T(8,128)(2,1)} %copy-done.26, f32[1024,768]{1,0:T(8,128)} %get-tuple-element.106, f32[768]{0:T(1024)S(1)} %copy-done.24, f32[768]{0:T(1024)S(1)} %reshape.416, f32[1024]{0:T(1024)S(1)} %copy-done.22, f32[1024]{0:T(1024)S(1)} %broadcast_multiply_fusion.4), kind=kOutput, calls=%fused_computation.13 | convolution fusion | flops 4838129664 | bytes 14170112 | tf_op jit(solution)/shard_map/dot_general | solution.py:403
  395.6 14.2 %collective-permute-done.16 = bf16[48,384]{1,0:T(8,128)(2,1)S(1)} collective-permute-done((bf16[48,384]{1,0:T(8,128)(2,1)S(1)}, bf16[48,384]{1,0:T(8,128)(2,1)S(1)}, u32[]{:S(2)}, u32[]{:S(2)}) %collective-permute-start.16) | collective-permute-done | bytes 36896 | tf_op jit(solution)/shard_map/ppermute | solution.py:32
  409.9 12.0 %collective-permute-done.17 = bf16[48,384]{1,0:T(8,128)(2,1)S(1)} collective-permute-done((bf16[48,384]{1,0:T(8,128)(2,1)S(1)}, bf16[48,384]{1,0:T(8,128)(2,1)S(1)}, u32[]{:S(2)}, u32[]{:S(2)}) %collective-permute-start.17) | collective-permute-done | bytes 36896 | tf_op jit(solution)/shard_map/ppermute | solution.py:32
  423.5 2.1 fusion.7
  429.9 2.3 fusion.5
  432.2 4.5 all-to-all-start.2
  439.3 12.4 %collective-permute-done.1 = bf16[1,192,2560]{2,1,0:T(8,128)(2,1)S(1)} collective-permute-done((bf16[1,192,2560]{2,1,0:T(8,128)(2,1)}, bf16[1,192,2560]{2,1,0:T(8,128)(2,1)S(1)}, u32[]{:S(2)}, u32[]{:S(2)}) %collective-permute-start.1) | collective-permute-done | bytes 983072 | tf_op jit(solution)/shard_map/ppermute | solution.py:45
  454.7 3.3 fusion.6
  461.0 13.6 %all-to-all-done.2 = bf16[8,128,768]{2,1,0:T(8,128)(2,1)} async-done(((bf16[8,128,768]{2,1,0:T(8,128)(2,1)}), bf16[8,128,768]{2,1,0:T(8,128)(2,1)}, u32[]{:S(2)}, u32[]{:S(2)}) %all-to-all-start.2) | async-done | bytes 1572896 | tf_op jit(solution)/shard_map/all_to_all | solution.py:23
  476.0 2.8 collective-permute-start.4
  482.4 1.6 collective-permute-start.32
  484.0 16.5 %collective-permute-done.21 = bf16[1,192,3072]{2,1,0:T(8,128)(2,1)} collective-permute-done((bf16[1,192,3072]{2,1,0:T(8,128)(2,1)}, bf16[1,192,3072]{2,1,0:T(8,128)(2,1)}, u32[]{:S(2)}, u32[]{:S(2)}) %collective-permute-start.21) | collective-permute-done | bytes 1179680 | tf_op jit(solution)/shard_map/ppermute | solution.py:45
  500.4 1.7 fusion.22
  504.6 2.1 collective-permute-start.8
  508.0 6.6 %collective-permute-done.7 = bf16[48,1280]{1,0:T(8,128)(2,1)S(1)} collective-permute-done((bf16[48,1280]{1,0:T(8,128)(2,1)S(1)}, bf16[48,1280]{1,0:T(8,128)(2,1)S(1)}, u32[]{:S(2)}, u32[]{:S(2)}) %collective-permute-start.7) | collective-permute-done | bytes 122912 | tf_op jit(solution)/shard_map/ppermute | solution.py:32
  516.8 1.9 collective-permute-start.33
  521.3 2.0 collective-permute-done.22
  524.3 5.9 collective-permute-done.9
  539.2 1.7 collective-permute-start.25
  541.5 2.3 collective-permute-start.37
  543.8 1.7 collective-permute-start.38
  545.4 2.5 collective-permute-done.25
  548.0 5.0 collective-permute-start.26
  553.1 2.4 collective-permute-start.28
  555.4 8.9 %collective-permute-done.37 = bf16[192,384]{1,0:T(8,128)(2,1)S(1)} collective-permute-done((bf16[192,384]{1,0:T(8,128)(2,1)S(1)}, bf16[192,384]{1,0:T(8,128)(2,1)S(1)}, u32[]{:S(2)}, u32[]{:S(2)}) %collective-permute-start.37) | collective-permute-done | bytes 147488 | tf_op jit(solution)/shard_map/ppermute | solution.py:32
  566.1 4.1 collective-permute-done.27
  573.3 6.2 %collective-permute-done.39 = bf16[768,384]{1,0:T(8,128)(2,1)S(1)} collective-permute-done((bf16[768,384]{1,0:T(8,128)(2,1)S(1)}, bf16[768,384]{1,0:T(8,128)(2,1)S(1)}, u32[]{:S(2)}, u32[]{:S(2)}) %collective-permute-start.39) | collective-permute-done | bytes 589856 | tf_op jit(solution)/shard_map/ppermute | solution.py:32
  581.6 5.6 collective-permute-done.29
  587.6 1.7 maximum_convert_fusion
  589.3 2.7 copy.47
  591.9 2.7 copy.48
  (277 shorter events, 95.6 us)
Async XLA Ops:
  7.2 70.3 %copy-start = (s32[8,1024]{1,0:T(8,128)S(1)}, s32[8,1024]{1,0:T(8,128)}, u32[]{:S(2)}) copy-start(s32[8,1024]{1,0:T(8,128)} %param.17) | copy-start | bytes 98308
  7.2 13.8 %copy-start.20 = (s32[8,2,12,3]{2,1,3,0:T(2,128)S(1)}, s32[8,2,12,3]{2,1,3,0:T(2,128)}, u32[]{:S(2)}) copy-start(s32[8,2,12,3]{2,1,3,0:T(2,128)} %param.18) | copy-start | bytes 6916
  7.2 27.5 %copy-start.12 = (bf16[8,128,768]{2,1,0:T(8,128)(2,1)S(1)}, bf16[8,128,768]{2,1,0:T(8,128)(2,1)}, u32[]{:S(2)}) copy-start(bf16[8,128,768]{2,1,0:T(8,128)(2,1)} %param.19) | copy-start | bytes 4718596
  7.2 74.9 %all-gather.12.cloned.1.call-start = ((), (), s32[]{:S(2)}) async-start(), calls=%async_computation.8 | async-start | bytes 4792320 | tf_op jit(solution)/shard_map/all_gather | solution.py:340
  19.5 159.6 %all-gather.6.cloned.1.call-start = ((), (), s32[]{:S(2)}) async-start(), calls=%async_computation.5 | async-start | bytes 1474560 | tf_op jit(solution)/shard_map/all_gather | solution.py:346
  20.2 166.9 %all-gather.8.cloned.1.call-start = ((), (), s32[]{:S(2)}) async-start(), calls=%async_computation.6 | async-start | bytes 5898240 | tf_op jit(solution)/shard_map/all_gather | solution.py:347
  73.0 40.1 %all-to-all-start = ((bf16[8,128,768]{2,1,0:T(8,128)(2,1)}), bf16[8,128,768]{2,1,0:T(8,128)(2,1)S(1)}, u32[]{:S(2)}, u32[]{:S(2)}) async-start(bf16[8,128,768]{2,1,0:T(8,128)(2,1)} %param.16), calls=%async_computation | async-start | bytes 3145728 | tf_op jit(solution)/shard_map/all_to_all | solution.py:23
  76.6 122.9 %all-gather.10.cloned.1.call-start = ((), (), s32[]{:S(2)}) async-start(), calls=%async_computation.7 | async-start | bytes 5898240 | tf_op jit(solution)/shard_map/all_gather | solution.py:348
  113.1 66.0 %copy-start.13 = (bf16[8,128,768]{2,1,0:T(8,128)(2,1)}, bf16[8,128,768]{2,1,0:T(8,128)(2,1)S(1)}, u32[]{:S(2)}) copy-start(bf16[8,128,768]{2,1,0:T(8,128)(2,1)S(1)} %all-to-all-done) | copy-start | bytes 4718596
  126.8 72.8 %copy-start.23 = (f32[768]{0:T(1024)}, f32[768]{0:T(1024)S(1)}, u32[]{:S(2)}) copy-start(f32[768]{0:T(1024)S(1)} %reshape.417) | copy-start | bytes 9220
  186.3 58.9 %copy-start.21 = (f32[1024]{0:T(1024)}, f32[1024]{0:T(1024)S(1)}, u32[]{:S(2)}) copy-start(f32[1024]{0:T(1024)S(1)} %add_rsqrt_fusion.1) | copy-start | bytes 12292
  212.8 9.3 %slice-start.4 = ((s8[4718592]{0:T(1024)(128)(4,1)}), s8[4194304]{0:T(1024)(128)(4,1)S(1)}, s32[]{:S(2)}) async-start(s8[4718592]{0:T(1024)(128)(4,1)} %bitcast.318), calls=%async_computation.13 | async-start | bytes 8388608
  214.6 7.5 %slice-start.5 = ((s8[4718592]{0:T(1024)(128)(4,1)}), s8[524288]{0:T(1024)(128)(4,1)S(1)}, s32[]{:S(2)}) async-start(s8[4718592]{0:T(1024)(128)(4,1)} %bitcast.318), calls=%async_computation.14 | async-start | bytes 1048576
  214.6 19.9 %slice-start.2 = ((s8[4718592]{0:T(1024)(128)(4,1)}), s8[4194304]{0:T(1024)(128)(4,1)S(1)}, s32[]{:S(2)}) async-start(s8[4718592]{0:T(1024)(128)(4,1)} %bitcast.316), calls=%async_computation.11 | async-start | bytes 8388608
  222.1 12.4 %slice-start.3 = ((s8[4718592]{0:T(1024)(128)(4,1)}), s8[524288]{0:T(1024)(128)(4,1)S(1)}, s32[]{:S(2)}) async-start(s8[4718592]{0:T(1024)(128)(4,1)} %bitcast.316), calls=%async_computation.12 | async-start | bytes 1048576
  234.5 10.7 %copy-start.26 = (bf16[1024,3072]{1,0:T(8,128)(2,1)}, bf16[1024,3072]{1,0:T(8,128)(2,1)S(1)}, u32[]{:S(2)}) copy-start(bf16[1024,3072]{1,0:T(8,128)(2,1)S(1)} %get-tuple-element.113) | copy-start | bytes 18874372
  328.7 7.2 %collective-permute-start.10 = (bf16[2,192,768]{2,1,0:T(8,128)(2,1)S(1)}, bf16[2,192,768]{2,1,0:T(8,128)(2,1)S(1)}, u32[]{:S(2)}, u32[]{:S(2)}) collective-permute-start(bf16[2,192,768]{2,1,0:T(8,128)(2,1)S(1)} %dynamic-slice_bitcast_fusion.2), channel_id=1, source_target_pairs={{0,8},{8,0},{16,24},{24,16},{1,9},{9,1},{17,25},{25,17},{2,10},{10... | collective-permute-start | bytes 1769480 | tf_op jit(solution)/shard_map/ppermute | solution.py:45
  337.0 12.2 %collective-permute-start.11 = (bf16[1,192,768]{2,1,0:T(8,128)(2,1)}, bf16[1,192,768]{2,1,0:T(8,128)(2,1)}, u32[]{:S(2)}, u32[]{:S(2)}) collective-permute-start(bf16[1,192,768]{2,1,0:T(8,128)(2,1)} %constant_dynamic-slice_fusion.2), channel_id=1, source_target_pairs={{0,16},{8,24},{16,0},{24,8},{1,17},{9,25},{17,1},{25,9},{2,18},{10... | collective-permute-start | bytes 884744 | tf_op jit(solution)/shard_map/ppermute | solution.py:45
  349.2 80.6 %collective-permute-start.30 = (bf16[2,768,768]{2,1,0:T(8,128)(2,1)}, bf16[2,768,768]{2,1,0:T(8,128)(2,1)}, u32[]{:S(2)}, u32[]{:S(2)}) collective-permute-start(bf16[2,768,768]{2,1,0:T(8,128)(2,1)} %dynamic-slice_bitcast_fusion), channel_id=1, source_target_pairs={{0,8},{8,0},{16,24},{24,16},{1,9},{9,1},{17,25},{25,17},{2,10},{10... | collective-permute-start | bytes 7077896 | tf_op jit(solution)/shard_map/ppermute | solution.py:45
  351.7 17.0 %collective-permute-start.12 = (bf16[192,384]{1,0:T(8,128)(2,1)}, bf16[192,384]{1,0:T(8,128)(2,1)}, u32[]{:S(2)}, u32[]{:S(2)}) collective-permute-start(bf16[192,384]{1,0:T(8,128)(2,1)} %fusion.70), channel_id=1, source_target_pairs={{0,1},{1,0},{2,3},{3,2},{4,5},{5,4},{6,7},{7,6},{8,9},{9,8},{10,11... | collective-permute-start | bytes 442376 | tf_op jit(solution)/shard_map/ppermute | solution.py:45
  368.6 8.3 %copy-start.7 = (bf16[4,192,256]{2,1,0:T(8,128)(2,1)}, bf16[4,192,256]{2,1,0:T(8,128)(2,1)S(1)}, u32[]{:S(2)}) copy-start(bf16[4,192,256]{2,1,0:T(8,128)(2,1)S(1)} %pad.4) | copy-start | bytes 1179652
  371.2 10.1 %collective-permute-start.13 = (bf16[48,384]{1,0:T(8,128)(2,1)}, bf16[48,384]{1,0:T(8,128)(2,1)}, u32[]{:S(2)}, u32[]{:S(2)}) collective-permute-start(bf16[48,384]{1,0:T(8,128)(2,1)} %get-tuple-element.96), channel_id=1, source_target_pairs={{0,2},{1,3},{2,0},{3,1},{4,6},{5,7},{6,4},{7,5},{8,10},{9,11},{10,... | collective-permute-start | bytes 110600 | tf_op jit(solution)/shard_map/ppermute | solution.py:45
  371.2 10.1 %collective-permute-start.14 = (bf16[48,384]{1,0:T(8,128)(2,1)}, bf16[48,384]{1,0:T(8,128)(2,1)}, u32[]{:S(2)}, u32[]{:S(2)}) collective-permute-start(bf16[48,384]{1,0:T(8,128)(2,1)} %get-tuple-element.98), channel_id=1, source_target_pairs={{0,4},{1,5},{2,6},{3,7},{4,0},{5,1},{6,2},{7,3},{8,12},{9,13},{10,... | collective-permute-start | bytes 110600 | tf_op jit(solution)/shard_map/ppermute | solution.py:45
  373.2 8.1 %collective-permute-start.15 = (bf16[48,384]{1,0:T(8,128)(2,1)}, bf16[48,384]{1,0:T(8,128)(2,1)}, u32[]{:S(2)}, u32[]{:S(2)}) collective-permute-start(bf16[48,384]{1,0:T(8,128)(2,1)} %get-tuple-element.97), channel_id=1, source_target_pairs={{0,6},{1,7},{2,4},{3,5},{4,2},{5,3},{6,0},{7,1},{8,14},{9,15},{10,... | collective-permute-start | bytes 110600 | tf_op jit(solution)/shard_map/ppermute | solution.py:45
  375.6 11.1 %copy-start.22 = (f32[1024]{0:T(1024)S(1)}, f32[1024]{0:T(1024)}, u32[]{:S(2)}) copy-start(f32[1024]{0:T(1024)} %copy-done.21) | copy-start | bytes 12292
  375.6 11.1 %copy-start.24 = (f32[768]{0:T(1024)S(1)}, f32[768]{0:T(1024)}, u32[]{:S(2)}) copy-start(f32[768]{0:T(1024)} %copy-done.23) | copy-start | bytes 9220
  377.0 46.6 %collective-permute-start = (bf16[2,192,2560]{2,1,0:T(8,128)(2,1)}, bf16[2,192,2560]{2,1,0:T(8,128)(2,1)}, u32[]{:S(2)}, u32[]{:S(2)}) collective-permute-start(bf16[2,192,2560]{2,1,0:T(8,128)(2,1)} %fusion.19), channel_id=1, source_target_pairs={{0,8},{8,0},{16,24},{24,16},{1,9},{9,1},{17,25},{25,17},{2,10},{10... | collective-permute-start | bytes 5898248 | tf_op jit(solution)/shard_map/ppermute | solution.py:45
  377.0 55.2 %all-to-all-start.4 = ((bf16[8,128,768]{2,1,0:T(8,128)(2,1)}), bf16[8,128,768]{2,1,0:T(8,128)(2,1)}, u32[]{:S(2)}, u32[]{:S(2)}) async-start(bf16[8,128,768]{2,1,0:T(8,128)(2,1)} %bitcast.288), calls=%async_computation.4 | async-start | bytes 3145728 | tf_op jit(solution)/shard_map/all_to_all | solution.py:23
  382.2 41.4 %copy-start.8 = (bf16[4,192,256]{2,1,0:T(8,128)(2,1)S(1)}, bf16[4,192,256]{2,1,0:T(8,128)(2,1)}, u32[]{:S(2)}) copy-start(bf16[4,192,256]{2,1,0:T(8,128)(2,1)} %copy-done.7) | copy-start | bytes 1179652
  382.2 27.7 %collective-permute-start.16 = (bf16[48,384]{1,0:T(8,128)(2,1)S(1)}, bf16[48,384]{1,0:T(8,128)(2,1)S(1)}, u32[]{:S(2)}, u32[]{:S(2)}) collective-permute-start(bf16[48,384]{1,0:T(8,128)(2,1)S(1)} %fusion.79), channel_id=1, source_target_pairs={{0,2},{1,3},{2,0},{3,1},{4,6},{5,7},{6,4},{7,5},{8,10},{9,11},{10,... | collective-permute-start | bytes 110600 | tf_op jit(solution)/shard_map/ppermute | solution.py:32
  384.1 37.7 %collective-permute-start.17 = (bf16[48,384]{1,0:T(8,128)(2,1)S(1)}, bf16[48,384]{1,0:T(8,128)(2,1)S(1)}, u32[]{:S(2)}, u32[]{:S(2)}) collective-permute-start(bf16[48,384]{1,0:T(8,128)(2,1)S(1)} %fusion.79), channel_id=1, source_target_pairs={{0,4},{1,5},{2,6},{3,7},{4,0},{5,1},{6,2},{7,3},{8,12},{9,13},{10,... | collective-permute-start | bytes 110600 | tf_op jit(solution)/shard_map/ppermute | solution.py:32
  386.5 35.4 %collective-permute-start.18 = (bf16[48,384]{1,0:T(8,128)(2,1)S(1)}, bf16[48,384]{1,0:T(8,128)(2,1)S(1)}, u32[]{:S(2)}, u32[]{:S(2)}) collective-permute-start(bf16[48,384]{1,0:T(8,128)(2,1)S(1)} %fusion.79), channel_id=1, source_target_pairs={{0,6},{1,7},{2,4},{3,5},{4,2},{5,3},{6,0},{7,1},{8,14},{9,15},{10,... | collective-permute-start | bytes 110600 | tf_op jit(solution)/shard_map/ppermute | solution.py:32
  395.6 31.7 %copy-start.6 = (bf16[768,3072]{1,0:T(8,128)(2,1)}, bf16[768,3072]{1,0:T(8,128)(2,1)S(1)}, u32[]{:S(2)}) copy-start(bf16[768,3072]{1,0:T(8,128)(2,1)S(1)} %convolution_convert_fusion.1) | copy-start | bytes 14155780
  422.0 6.8 %collective-permute-start.19 = (bf16[192,384]{1,0:T(8,128)(2,1)S(1)}, bf16[192,384]{1,0:T(8,128)(2,1)S(1)}, u32[]{:S(2)}, u32[]{:S(2)}) collective-permute-start(bf16[192,384]{1,0:T(8,128)(2,1)S(1)} %get-tuple-element.90), channel_id=1, source_target_pairs={{0,1},{1,0},{2,3},{3,2},{4,5},{5,4},{6,7},{7,6},{8,9},{9,8},{10,11... | collective-permute-start | bytes 442376 | tf_op jit(solution)/shard_map/ppermute | solution.py:32
  426.7 24.9 %collective-permute-start.1 = (bf16[1,192,2560]{2,1,0:T(8,128)(2,1)}, bf16[1,192,2560]{2,1,0:T(8,128)(2,1)S(1)}, u32[]{:S(2)}, u32[]{:S(2)}) collective-permute-start(bf16[1,192,2560]{2,1,0:T(8,128)(2,1)} %constant_dynamic-slice_fusion.3), channel_id=1, source_target_pairs={{0,16},{8,24},{16,0},{24,8},{1,17},{9,25},{17,1},{25,9},{2,18},{10... | collective-permute-start | bytes 2949128 | tf_op jit(solution)/shard_map/ppermute | solution.py:45
  428.8 25.8 %collective-permute-start.20 = (bf16[2,192,3072]{2,1,0:T(8,128)(2,1)}, bf16[2,192,3072]{2,1,0:T(8,128)(2,1)}, u32[]{:S(2)}, u32[]{:S(2)}) collective-permute-start(bf16[2,192,3072]{2,1,0:T(8,128)(2,1)} %dynamic-slice_bitcast_fusion.1), channel_id=1, source_target_pairs={{0,8},{8,0},{16,24},{24,16},{1,9},{9,1},{17,25},{25,17},{2,10},{10... | collective-permute-start | bytes 7077896 | tf_op jit(solution)/shard_map/ppermute | solution.py:45
  432.2 42.5 %all-to-all-start.2 = ((bf16[8,128,768]{2,1,0:T(8,128)(2,1)}), bf16[8,128,768]{2,1,0:T(8,128)(2,1)}, u32[]{:S(2)}, u32[]{:S(2)}) async-start(bf16[8,128,768]{2,1,0:T(8,128)(2,1)} %bitcast.264), calls=%async_computation.2 | async-start | bytes 3145728 | tf_op jit(solution)/shard_map/all_to_all | solution.py:23
  437.8 42.6 %collective-permute-start.31 = (bf16[1,768,768]{2,1,0:T(8,128)(2,1)}, bf16[1,768,768]{2,1,0:T(8,128)(2,1)}, u32[]{:S(2)}, u32[]{:S(2)}) collective-permute-start(bf16[1,768,768]{2,1,0:T(8,128)(2,1)} %constant_dynamic-slice_fusion), channel_id=1, source_target_pairs={{0,16},{8,24},{16,0},{24,8},{1,17},{9,25},{17,1},{25,9},{2,18},{10... | collective-permute-start | bytes 3538952 | tf_op jit(solution)/shard_map/ppermute | solution.py:45
  454.1 20.5 %collective-permute-start.2 = (bf16[192,1280]{1,0:T(8,128)(2,1)}, bf16[192,1280]{1,0:T(8,128)(2,1)}, u32[]{:S(2)}, u32[]{:S(2)}) collective-permute-start(bf16[192,1280]{1,0:T(8,128)(2,1)} %fusion.51), channel_id=1, source_target_pairs={{0,1},{1,0},{2,3},{3,2},{4,5},{5,4},{6,7},{7,6},{8,9},{9,8},{10,11... | collective-permute-start | bytes 1474568 | tf_op jit(solution)/shard_map/ppermute | solution.py:45
  460.4 40.0 %collective-permute-start.21 = (bf16[1,192,3072]{2,1,0:T(8,128)(2,1)}, bf16[1,192,3072]{2,1,0:T(8,128)(2,1)}, u32[]{:S(2)}, u32[]{:S(2)}) collective-permute-start(bf16[1,192,3072]{2,1,0:T(8,128)(2,1)} %constant_dynamic-slice_fusion.1), channel_id=1, source_target_pairs={{0,16},{8,24},{16,0},{24,8},{1,17},{9,25},{17,1},{25,9},{2,18},{10... | collective-permute-start | bytes 3538952 | tf_op jit(solution)/shard_map/ppermute | solution.py:45
  475.9 26.2 %collective-permute-start.3 = (bf16[48,1280]{1,0:T(8,128)(2,1)S(1)}, bf16[48,1280]{1,0:T(8,128)(2,1)S(1)}, u32[]{:S(2)}, u32[]{:S(2)}) collective-permute-start(bf16[48,1280]{1,0:T(8,128)(2,1)S(1)} %get-tuple-element.83), channel_id=1, source_target_pairs={{0,2},{1,3},{2,0},{3,1},{4,6},{5,7},{6,4},{7,5},{8,10},{9,11},{10,... | collective-permute-start | bytes 368648 | tf_op jit(solution)/shard_map/ppermute | solution.py:45
  476.0 26.2 %collective-permute-start.4 = (bf16[48,1280]{1,0:T(8,128)(2,1)S(1)}, bf16[48,1280]{1,0:T(8,128)(2,1)S(1)}, u32[]{:S(2)}, u32[]{:S(2)}) collective-permute-start(bf16[48,1280]{1,0:T(8,128)(2,1)S(1)} %get-tuple-element.85), channel_id=1, source_target_pairs={{0,4},{1,5},{2,6},{3,7},{4,0},{5,1},{6,2},{7,3},{8,12},{9,13},{10,... | collective-permute-start | bytes 368648 | tf_op jit(solution)/shard_map/ppermute | solution.py:45
  478.9 21.5 %copy-start.3 = (bf16[2,192,3072]{2,1,0:T(8,128)(2,1)S(1)}, bf16[2,192,3072]{2,1,0:T(8,128)(2,1)}, u32[]{:S(2)}) copy-start(bf16[2,192,3072]{2,1,0:T(8,128)(2,1)} %copy-done.2) | copy-start | bytes 7077892
  478.9 23.3 %collective-permute-start.5 = (bf16[48,1280]{1,0:T(8,128)(2,1)S(1)}, bf16[48,1280]{1,0:T(8,128)(2,1)S(1)}, u32[]{:S(2)}, u32[]{:S(2)}) collective-permute-start(bf16[48,1280]{1,0:T(8,128)(2,1)S(1)} %get-tuple-element.84), channel_id=1, source_target_pairs={{0,6},{1,7},{2,4},{3,5},{4,2},{5,3},{6,0},{7,1},{8,14},{9,15},{10,... | collective-permute-start | bytes 368648 | tf_op jit(solution)/shard_map/ppermute | solution.py:45
  482.4 33.4 %collective-permute-start.32 = (bf16[768,384]{1,0:T(8,128)(2,1)S(1)}, bf16[768,384]{1,0:T(8,128)(2,1)S(1)}, u32[]{:S(2)}, u32[]{:S(2)}) collective-permute-start(bf16[768,384]{1,0:T(8,128)(2,1)S(1)} %fusion.34), channel_id=1, source_target_pairs={{0,1},{1,0},{2,3},{3,2},{4,5},{5,4},{6,7},{7,6},{8,9},{9,8},{10,11... | collective-permute-start | bytes 1769480 | tf_op jit(solution)/shard_map/ppermute | solution.py:45
  502.3 5.7 collective-permute-start.6
  503.6 11.0 %collective-permute-start.7 = (bf16[48,1280]{1,0:T(8,128)(2,1)S(1)}, bf16[48,1280]{1,0:T(8,128)(2,1)S(1)}, u32[]{:S(2)}, u32[]{:S(2)}) collective-permute-start(bf16[48,1280]{1,0:T(8,128)(2,1)S(1)} %fusion.64), channel_id=1, source_target_pairs={{0,4},{1,5},{2,6},{3,7},{4,0},{5,1},{6,2},{7,3},{8,12},{9,13},{10,... | collective-permute-start | bytes 368648 | tf_op jit(solution)/shard_map/ppermute | solution.py:32
  504.6 10.0 %collective-permute-start.8 = (bf16[48,1280]{1,0:T(8,128)(2,1)S(1)}, bf16[48,1280]{1,0:T(8,128)(2,1)S(1)}, u32[]{:S(2)}, u32[]{:S(2)}) collective-permute-start(bf16[48,1280]{1,0:T(8,128)(2,1)S(1)} %fusion.64), channel_id=1, source_target_pairs={{0,6},{1,7},{2,4},{3,5},{4,2},{5,3},{6,0},{7,1},{8,14},{9,15},{10,... | collective-permute-start | bytes 368648 | tf_op jit(solution)/shard_map/ppermute | solution.py:32
  507.0 16.3 %collective-permute-start.22 = (bf16[192,1536]{1,0:T(8,128)(2,1)S(1)}, bf16[192,1536]{1,0:T(8,128)(2,1)S(1)}, u32[]{:S(2)}, u32[]{:S(2)}) collective-permute-start(bf16[192,1536]{1,0:T(8,128)(2,1)S(1)} %fusion.42), channel_id=1, source_target_pairs={{0,1},{1,0},{2,3},{3,2},{4,5},{5,4},{6,7},{7,6},{8,9},{9,8},{10,11... | collective-permute-start | bytes 1769480 | tf_op jit(solution)/shard_map/ppermute | solution.py:45
  514.8 15.4 %collective-permute-start.9 = (bf16[192,1280]{1,0:T(8,128)(2,1)S(1)}, bf16[192,1280]{1,0:T(8,128)(2,1)S(1)}, u32[]{:S(2)}, u32[]{:S(2)}) collective-permute-start(bf16[192,1280]{1,0:T(8,128)(2,1)S(1)} %get-tuple-element.77), channel_id=1, source_target_pairs={{0,1},{1,0},{2,3},{3,2},{4,5},{5,4},{6,7},{7,6},{8,9},{9,8},{10,11... | collective-permute-start | bytes 1474568 | tf_op jit(solution)/shard_map/ppermute | solution.py:32
  516.8 22.4 %collective-permute-start.33 = (bf16[192,384]{1,0:T(8,128)(2,1)}, bf16[192,384]{1,0:T(8,128)(2,1)S(1)}, u32[]{:S(2)}, u32[]{:S(2)}) collective-permute-start(bf16[192,384]{1,0:T(8,128)(2,1)} %get-tuple-element.65), channel_id=1, source_target_pairs={{0,2},{1,3},{2,0},{3,1},{4,6},{5,7},{6,4},{7,5},{8,10},{9,11},{10,... | collective-permute-start | bytes 442376 | tf_op jit(solution)/shard_map/ppermute | solution.py:45
  518.7 22.2 %collective-permute-start.34 = (bf16[192,384]{1,0:T(8,128)(2,1)S(1)}, bf16[192,384]{1,0:T(8,128)(2,1)S(1)}, u32[]{:S(2)}, u32[]{:S(2)}) collective-permute-start(bf16[192,384]{1,0:T(8,128)(2,1)S(1)} %get-tuple-element.67), channel_id=1, source_target_pairs={{0,4},{1,5},{2,6},{3,7},{4,0},{5,1},{6,2},{7,3},{8,12},{9,13},{10,... | collective-permute-start | bytes 442376 | tf_op jit(solution)/shard_map/ppermute | solution.py:45
  519.9 21.0 %collective-permute-start.35 = (bf16[192,384]{1,0:T(8,128)(2,1)S(1)}, bf16[192,384]{1,0:T(8,128)(2,1)S(1)}, u32[]{:S(2)}, u32[]{:S(2)}) collective-permute-start(bf16[192,384]{1,0:T(8,128)(2,1)S(1)} %get-tuple-element.66), channel_id=1, source_target_pairs={{0,6},{1,7},{2,4},{3,5},{4,2},{5,3},{6,0},{7,1},{8,14},{9,15},{10,... | collective-permute-start | bytes 442376 | tf_op jit(solution)/shard_map/ppermute | solution.py:45
  524.3 19.5 %collective-permute-start.23 = (bf16[48,1536]{1,0:T(8,128)(2,1)}, bf16[48,1536]{1,0:T(8,128)(2,1)S(1)}, u32[]{:S(2)}, u32[]{:S(2)}) collective-permute-start(bf16[48,1536]{1,0:T(8,128)(2,1)} %get-tuple-element.74), channel_id=1, source_target_pairs={{0,2},{1,3},{2,0},{3,1},{4,6},{5,7},{6,4},{7,5},{8,10},{9,11},{10,... | collective-permute-start | bytes 442376 | tf_op jit(solution)/shard_map/ppermute | solution.py:45
  530.2 15.2 %collective-permute-start.24 = (bf16[48,1536]{1,0:T(8,128)(2,1)S(1)}, bf16[48,1536]{1,0:T(8,128)(2,1)S(1)}, u32[]{:S(2)}, u32[]{:S(2)}) collective-permute-start(bf16[48,1536]{1,0:T(8,128)(2,1)S(1)} %get-tuple-element.76), channel_id=1, source_target_pairs={{0,4},{1,5},{2,6},{3,7},{4,0},{5,1},{6,2},{7,3},{8,12},{9,13},{10,... | collective-permute-start | bytes 442376 | tf_op jit(solution)/shard_map/ppermute | solution.py:45
  539.2 8.7 %collective-permute-start.25 = (bf16[48,1536]{1,0:T(8,128)(2,1)S(1)}, bf16[48,1536]{1,0:T(8,128)(2,1)S(1)}, u32[]{:S(2)}, u32[]{:S(2)}) collective-permute-start(bf16[48,1536]{1,0:T(8,128)(2,1)S(1)} %get-tuple-element.75), channel_id=1, source_target_pairs={{0,6},{1,7},{2,4},{3,5},{4,2},{5,3},{6,0},{7,1},{8,14},{9,15},{10,... | collective-permute-start | bytes 442376 | tf_op jit(solution)/shard_map/ppermute | solution.py:45
  541.0 12.1 %collective-permute-start.36 = (bf16[192,384]{1,0:T(8,128)(2,1)S(1)}, bf16[192,384]{1,0:T(8,128)(2,1)S(1)}, u32[]{:S(2)}, u32[]{:S(2)}) collective-permute-start(bf16[192,384]{1,0:T(8,128)(2,1)S(1)} %fusion.57), channel_id=1, source_target_pairs={{0,2},{1,3},{2,0},{3,1},{4,6},{5,7},{6,4},{7,5},{8,10},{9,11},{10,... | collective-permute-start | bytes 442376 | tf_op jit(solution)/shard_map/ppermute | solution.py:32
  541.5 22.8 %collective-permute-start.37 = (bf16[192,384]{1,0:T(8,128)(2,1)S(1)}, bf16[192,384]{1,0:T(8,128)(2,1)S(1)}, u32[]{:S(2)}, u32[]{:S(2)}) collective-permute-start(bf16[192,384]{1,0:T(8,128)(2,1)S(1)} %fusion.57), channel_id=1, source_target_pairs={{0,4},{1,5},{2,6},{3,7},{4,0},{5,1},{6,2},{7,3},{8,12},{9,13},{10,... | collective-permute-start | bytes 442376 | tf_op jit(solution)/shard_map/ppermute | solution.py:32
  543.8 20.5 %collective-permute-start.38 = (bf16[192,384]{1,0:T(8,128)(2,1)S(1)}, bf16[192,384]{1,0:T(8,128)(2,1)S(1)}, u32[]{:S(2)}, u32[]{:S(2)}) collective-permute-start(bf16[192,384]{1,0:T(8,128)(2,1)S(1)} %fusion.57), channel_id=1, source_target_pairs={{0,6},{1,7},{2,4},{3,5},{4,2},{5,3},{6,0},{7,1},{8,14},{9,15},{10,... | collective-permute-start | bytes 442376 | tf_op jit(solution)/shard_map/ppermute | solution.py:32
  548.0 18.1 %collective-permute-start.26 = (bf16[48,1536]{1,0:T(8,128)(2,1)S(1)}, bf16[48,1536]{1,0:T(8,128)(2,1)S(1)}, u32[]{:S(2)}, u32[]{:S(2)}) collective-permute-start(bf16[48,1536]{1,0:T(8,128)(2,1)S(1)} %fusion.60), channel_id=1, source_target_pairs={{0,2},{1,3},{2,0},{3,1},{4,6},{5,7},{6,4},{7,5},{8,10},{9,11},{10,... | collective-permute-start | bytes 442376 | tf_op jit(solution)/shard_map/ppermute | solution.py:32
  553.0 17.3 %collective-permute-start.27 = (bf16[48,1536]{1,0:T(8,128)(2,1)S(1)}, bf16[48,1536]{1,0:T(8,128)(2,1)S(1)}, u32[]{:S(2)}, u32[]{:S(2)}) collective-permute-start(bf16[48,1536]{1,0:T(8,128)(2,1)S(1)} %fusion.60), channel_id=1, source_target_pairs={{0,4},{1,5},{2,6},{3,7},{4,0},{5,1},{6,2},{7,3},{8,12},{9,13},{10,... | collective-permute-start | bytes 442376 | tf_op jit(solution)/shard_map/ppermute | solution.py:32
  553.1 17.2 %collective-permute-start.28 = (bf16[48,1536]{1,0:T(8,128)(2,1)S(1)}, bf16[48,1536]{1,0:T(8,128)(2,1)S(1)}, u32[]{:S(2)}, u32[]{:S(2)}) collective-permute-start(bf16[48,1536]{1,0:T(8,128)(2,1)S(1)} %fusion.60), channel_id=1, source_target_pairs={{0,6},{1,7},{2,4},{3,5},{4,2},{5,3},{6,0},{7,1},{8,14},{9,15},{10,... | collective-permute-start | bytes 442376 | tf_op jit(solution)/shard_map/ppermute | solution.py:32
  564.6 15.0 %collective-permute-start.39 = (bf16[768,384]{1,0:T(8,128)(2,1)S(1)}, bf16[768,384]{1,0:T(8,128)(2,1)S(1)}, u32[]{:S(2)}, u32[]{:S(2)}) collective-permute-start(bf16[768,384]{1,0:T(8,128)(2,1)S(1)} %get-tuple-element.59), channel_id=1, source_target_pairs={{0,1},{1,0},{2,3},{3,2},{4,5},{5,4},{6,7},{7,6},{8,9},{9,8},{10,11... | collective-permute-start | bytes 1769480 | tf_op jit(solution)/shard_map/ppermute | solution.py:32
  570.5 16.7 %collective-permute-start.29 = (bf16[192,1536]{1,0:T(8,128)(2,1)S(1)}, bf16[192,1536]{1,0:T(8,128)(2,1)S(1)}, u32[]{:S(2)}, u32[]{:S(2)}) collective-permute-start(bf16[192,1536]{1,0:T(8,128)(2,1)S(1)} %get-tuple-element.68), channel_id=1, source_target_pairs={{0,1},{1,0},{2,3},{3,2},{4,5},{5,4},{6,7},{7,6},{8,9},{9,8},{10,11... | collective-permute-start | bytes 1769480 | tf_op jit(solution)/shard_map/ppermute | solution.py:32
  (19 other events, 66.7 us)
Sparse Core Ops, SparseCore 0:
  19.6 35.1 all-gather.11
  56.3 17.4 all-gather.5
  75.4 37.4 all-gather.7
  114.3 37.4 all-gather.9
